TPU v7x, 512 devices: a whole 4x4x16 slice. The times are simulated.
512 devices in a mesh: tm: 32 (over x, y, core), space: 16 (over z).
Axes of the slice: x: 4, y: 4, z: 16, core: 2. Of those that a mesh axis runs over, the one named last changes fastest.
Arguments:
- latent: float32 [128, 512, 1024], P('tm', 'space'), may hold values from -3 to 3
- counts: int32 [128, 512, 1024], P('tm', 'space'), may hold values from 0 to 6
- exposure: float32 [128, 512, 1024], P('tm', 'space'), may hold values from 0.5 to 6, as said below
- region_ids: int32 [128], P('space'), may hold values from 0 to 15
- coefficients: float32 [16], replicated, may hold values from -2 to 2
Outputs:
- updated: float32 [128, 512, 1024], P('tm', 'space')
- residual: float32 [128, 512, 1024], P('tm', 'space')
Inputs may be any that keep to these rules, and one draw needn't show every extreme that they name: exposure is positive.
All inputs are finite; a program needn't handle non-finite values.
Results may differ from a plain program's by a relative error of at most 0.00013.
Values sent between devices are 32-bit elements; how exact they have to be, the bound alone decides.
No kernel may reach another device: no remote copies, remote signals or barrier semaphores. Data moves between devices by JAX's collectives and lax.ppermute only.
A program may use at most 64 MiB of HBM per device.

v0:
```python
import jax
import jax.numpy as jnp
from jax import lax
from jax.sharding import PartitionSpec as P

ITERS = 2


kappa_square = 0.3
time_corr = 0.9
prior_scale = 0.05


def padded_2(cells, sides, width):
    for axis, dim in sides:
        count = lax.axis_size(axis)
        ends = count - 1
        head = lax.slice_in_dim(cells, 0, width, axis=dim)
        tail = lax.slice_in_dim(cells, cells.shape[dim] - width, cells.shape[dim], axis=dim)
        cells = jnp.concatenate(
            [
                lax.ppermute(tail, axis, [(i, (i + 1) % count) for i in range(ends)]),
                cells,
                lax.ppermute(head, axis, [((i + 1) % count, i) for i in range(ends)]),
            ],
            axis=dim,
        )
    return cells


def stiffness_rows(extended):
    padded = jnp.pad(extended, ((0, 0), (0, 0), (1, 1)))
    neighbours = (
        extended[:, 2:, :] + extended[:, :-2, :] + padded[:, 1:-1, 2:] + padded[:, 1:-1, :-2]
    )
    return (kappa_square + 4.0) * extended[:, 1:-1, :] - neighbours


def couple(center, earlier_days, later_days):
    day_count = center.shape[0]
    day_index = lax.axis_index("tm") * day_count + jnp.arange(day_count)
    all_days = day_count * lax.axis_size("tm")
    weight = jnp.where(
        (day_index == 0) | (day_index == all_days - 1), 1.0, 1.0 + time_corr * time_corr
    )
    weight = weight.astype(jnp.float32)[:, None, None]
    return prior_scale * (weight * center - time_corr * (earlier_days + later_days))


def precision(field):
    once_applied = stiffness_rows(padded_2(field, (("space", 1),), 1))
    spatial = stiffness_rows(padded_2(once_applied, (("space", 1),), 1))
    neighbour_days = padded_2(spatial, (("tm", 0),), 1)
    return couple(spatial, neighbour_days[:-2], neighbour_days[2:])


def squares(residual):
    return lax.psum(jnp.sum(residual * residual), ("tm", "space"))


def body(latent, counts, exposure, region_ids, coefficients):
    row_count = latent.shape[1]
    blocks = region_ids.shape[0]
    one_hot = (region_ids[:, None] == jnp.arange(coefficients.shape[0])[None, :]).astype(
        jnp.float32
    )
    block_offset = jnp.sum(one_hot * coefficients[None, :], axis=1)
    offset = jnp.broadcast_to(block_offset[:, None], (blocks, row_count // blocks)).reshape(
        row_count
    )
    intensity = exposure * jnp.exp(offset[None, :, None] + latent)
    gradient = precision(latent) - counts.astype(jnp.float32) + intensity
    newton_step = jnp.zeros_like(latent)
    residual = -gradient
    direction = residual
    norm_now = squares(residual)
    for iteration in range(ITERS):
        image_vec = precision(direction) + intensity * direction
        curvature = lax.psum(jnp.sum(direction * image_vec), ("tm", "space"))
        step_size = norm_now / curvature
        newton_step = newton_step + step_size * direction
        residual = residual - step_size * image_vec
        if iteration + 1 < ITERS:
            norm_next = squares(residual)
            direction = residual + norm_next / norm_now * direction
            norm_now = norm_next
    return (latent + newton_step, residual)


def solution(mesh):
    return jax.shard_map(
        body,
        mesh=mesh,
        in_specs=(
            P("tm", "space", None),
            P("tm", "space", None),
            P("tm", "space", None),
            P("space"),
            P(),
        ),
        out_specs=(P("tm", "space", None), P("tm", "space", None)),
        check_vma=False,
    )
```

profile of v0, /device:TPU:1, one launch (start us, length us, event | category | flops | bytes accessed | tf_op | source)
XLA Modules:
  0.0 413.9 jit_solution(17777879429659316694)
XLA Ops:
  0.6 1.0 fusion.40
  1.6 4.4 %collective-permute-start.1 = (f32[4,1,1024]{2,1,0:T(1,128)S(1)}, f32[4,1,1024]{2,1,0:T(1,128)S(1)}, u32[]{:S(2)}, u32[]{:S(2)}) collective-permute-start(f32[4,1,1024]{2,1,0:T(1,128)S(1)} %get-tuple-element.28), channel_id=1, source_target_pairs={{0,1},{1,2},{2,3},{3,4},{4,5},{5,6},{6,7},{7,8},{8,9},{9,10},{10,1... | collective-permute-start | bytes 49160 | tf_op jit(solution)/shard_map/ppermute | solution.py:22
  6.0 1.4 collective-permute-start
  7.5 3.4 collective-permute-done
  10.8 1.4 select_maximum_fusion.10
  12.2 0.3 fusion.27
  12.6 3.8 collective-permute-start.3
  16.4 1.3 collective-permute-start.2
  17.7 4.3 %collective-permute-done.2 = f32[4,1,1024]{2,1,0:T(1,128)S(1)} collective-permute-done((f32[4,1,1024]{2,1,0:T(1,128)S(1)}, f32[4,1,1024]{2,1,0:T(1,128)S(1)}, u32[]{:S(2)}, u32[]{:S(2)}) %collective-permute-start.2) | collective-permute-done | bytes 16416 | tf_op jit(solution)/shard_map/ppermute | solution.py:24
  22.0 0.3 select_maximum_fusion.8
  22.4 0.3 fusion.25
  22.7 6.2 %collective-permute-start.4 = (f32[1,32,1024]{2,1,0:T(8,128)S(1)}, f32[1,32,1024]{2,1,0:T(8,128)S(1)}, u32[]{:S(2)}, u32[]{:S(2)}) collective-permute-start(f32[1,32,1024]{2,1,0:T(8,128)S(1)} %get-tuple-element.24), channel_id=1, source_target_pairs={{0,16},{16,32},{32,48},{48,64},{64,80},{80,96},{96,112},{112,128},... | collective-permute-start | bytes 393224 | tf_op jit(solution)/shard_map/ppermute | solution.py:22
  28.9 1.9 collective-permute-start.5
  31.3 4.0 collective-permute-done.5
  35.2 0.3 fusion.30
  35.6 4.8 %collective-permute-start.7 = (f32[4,1,1024]{2,1,0:T(1,128)S(1)}, f32[4,1,1024]{2,1,0:T(1,128)S(1)}, u32[]{:S(2)}, u32[]{:S(2)}) collective-permute-start(f32[4,1,1024]{2,1,0:T(1,128)S(1)} %get-tuple-element.22), channel_id=1, source_target_pairs={{0,1},{1,2},{2,3},{3,4},{4,5},{5,6},{6,7},{7,8},{8,9},{9,10},{10,1... | collective-permute-start | bytes 49160 | tf_op jit(solution)/shard_map/ppermute | solution.py:22
  40.5 1.3 collective-permute-start.6
  41.8 3.5 collective-permute-done.6
  45.2 0.3 select_maximum_fusion.6
  45.6 0.3 fusion.17
  46.0 3.5 collective-permute-start.9
  49.5 1.3 collective-permute-start.8
  50.8 3.2 collective-permute-done.8
  54.0 0.3 select_maximum_fusion.4
  54.3 0.3 fusion.15
  54.7 4.5 %collective-permute-start.10 = (f32[1,32,1024]{2,1,0:T(8,128)S(1)}, f32[1,32,1024]{2,1,0:T(8,128)S(1)}, u32[]{:S(2)}, u32[]{:S(2)}) collective-permute-start(f32[1,32,1024]{2,1,0:T(8,128)S(1)} %get-tuple-element.18), channel_id=1, source_target_pairs={{0,16},{16,32},{32,48},{48,64},{64,80},{80,96},{96,112},{112,128},... | collective-permute-start | bytes 393224 | tf_op jit(solution)/shard_map/ppermute | solution.py:22
  59.1 1.9 collective-permute-start.11
  61.1 4.3 %collective-permute-done.11 = f32[1,32,1024]{2,1,0:T(8,128)S(1)} collective-permute-done((f32[1,32,1024]{2,1,0:T(8,128)S(1)}, f32[1,32,1024]{2,1,0:T(8,128)S(1)}, u32[]{:S(2)}, u32[]{:S(2)}) %collective-permute-start.11) | collective-permute-done | bytes 131104 | tf_op jit(solution)/shard_map/ppermute | solution.py:24
  65.4 1.1 multiply_reduce_fusion.2
  66.5 108.6 %all-reduce.6 = (f32[]{:T(128)}, f32[]{:T(128)}) all-reduce(f32[]{:T(128)} %get-tuple-element.3, f32[]{:T(128)} %get-tuple-element.2), channel_id=1, replica_groups=mesh['tm'=32,'space'=16] {'tm','space'}, use_global_device_ids=true, to_apply=%region_2.3 | all-reduce | flops 2 | bytes 16 | tf_op jit(solution)/shard_map/psum | solution.py:58
  176.4 0.7 multiply_reduce_fusion.1
  177.2 98.6 %psum.30 = f32[]{:T(128)} all-reduce(f32[]{:T(128)} %multiply_reduce_fusion.1), channel_id=1, replica_groups=mesh['tm'=32,'space'=16] {'tm','space'}, use_global_device_ids=true, to_apply=%region_6.7 | all-reduce | flops 1 | bytes 8 | tf_op jit(solution)/shard_map/psum | solution.py:58
  277.3 3.7 collective-permute-start.13
  280.9 1.3 collective-permute-start.12
  282.3 3.2 collective-permute-done.12
  285.4 0.3 select_maximum_fusion.2
  285.8 0.3 fusion.8
  286.1 2.7 collective-permute-start.15
  288.8 1.3 collective-permute-start.14
  290.1 3.2 collective-permute-done.14
  293.3 0.3 select_maximum_fusion
  293.7 0.3 fusion.6
  294.0 6.1 %collective-permute-start.16 = (f32[1,32,1024]{2,1,0:T(8,128)S(1)}, f32[1,32,1024]{2,1,0:T(8,128)S(1)}, u32[]{:S(2)}, u32[]{:S(2)}) collective-permute-start(f32[1,32,1024]{2,1,0:T(8,128)S(1)} %get-tuple-element.12), channel_id=1, source_target_pairs={{0,16},{16,32},{32,48},{48,64},{64,80},{80,96},{96,112},{112,128},... | collective-permute-start | bytes 393224 | tf_op jit(solution)/shard_map/ppermute | solution.py:22
  300.1 1.9 collective-permute-start.17
  302.0 4.3 %collective-permute-done.17 = f32[1,32,1024]{2,1,0:T(8,128)S(1)} collective-permute-done((f32[1,32,1024]{2,1,0:T(8,128)S(1)}, f32[1,32,1024]{2,1,0:T(8,128)S(1)}, u32[]{:S(2)}, u32[]{:S(2)}) %collective-permute-start.17) | collective-permute-done | bytes 131104 | tf_op jit(solution)/shard_map/ppermute | solution.py:24
  306.4 0.9 multiply_reduce_fusion
  307.3 103.9 %psum.31 = f32[]{:T(128)} all-reduce(f32[]{:T(128)} %multiply_reduce_fusion), channel_id=1, replica_groups=mesh['tm'=32,'space'=16] {'tm','space'}, use_global_device_ids=true, to_apply=%region_8.9 | all-reduce | flops 1 | bytes 8 | tf_op jit(solution)/shard_map/psum | solution.py:79
  412.5 1.4 multiply_subtract_fusion
  (32 shorter events, 0.7 us)
Async XLA Ops:
  1.6 5.8 %collective-permute-start.1 = (f32[4,1,1024]{2,1,0:T(1,128)S(1)}, f32[4,1,1024]{2,1,0:T(1,128)S(1)}, u32[]{:S(2)}, u32[]{:S(2)}) collective-permute-start(f32[4,1,1024]{2,1,0:T(1,128)S(1)} %get-tuple-element.28), channel_id=1, source_target_pairs={{0,1},{1,2},{2,3},{3,4},{4,5},{5,6},{6,7},{7,8},{8,9},{9,10},{10,1... | collective-permute-start | bytes 49160 | tf_op jit(solution)/shard_map/ppermute | solution.py:22
  6.0 6.2 %copy-start = (f32[4,32,1024]{2,1,0:T(8,128)S(1)}, f32[4,32,1024]{2,1,0:T(8,128)}, u32[]{:S(2)}) copy-start(f32[4,32,1024]{2,1,0:T(8,128)} %param.5) | copy-start | bytes 1572868
  6.0 4.8 %collective-permute-start = (f32[4,1,1024]{2,1,0:T(1,128)S(1)}, f32[4,1,1024]{2,1,0:T(1,128)S(1)}, u32[]{:S(2)}, u32[]{:S(2)}) collective-permute-start(f32[4,1,1024]{2,1,0:T(1,128)S(1)} %get-tuple-element.29), channel_id=1, source_target_pairs={{1,0},{2,1},{3,2},{4,3},{5,4},{6,5},{7,6},{8,7},{9,8},{10,9},{11,1... | collective-permute-start | bytes 49160 | tf_op jit(solution)/shard_map/ppermute | solution.py:24
  12.6 5.1 %collective-permute-start.3 = (f32[4,1,1024]{2,1,0:T(1,128)S(1)}, f32[4,1,1024]{2,1,0:T(1,128)S(1)}, u32[]{:S(2)}, u32[]{:S(2)}) collective-permute-start(f32[4,1,1024]{2,1,0:T(1,128)S(1)} %get-tuple-element.26), channel_id=1, source_target_pairs={{0,1},{1,2},{2,3},{3,4},{4,5},{5,6},{6,7},{7,8},{8,9},{9,10},{10,1... | collective-permute-start | bytes 49160 | tf_op jit(solution)/shard_map/ppermute | solution.py:22
  16.4 5.6 %collective-permute-start.2 = (f32[4,1,1024]{2,1,0:T(1,128)S(1)}, f32[4,1,1024]{2,1,0:T(1,128)S(1)}, u32[]{:S(2)}, u32[]{:S(2)}) collective-permute-start(f32[4,1,1024]{2,1,0:T(1,128)S(1)} %get-tuple-element.27), channel_id=1, source_target_pairs={{1,0},{2,1},{3,2},{4,3},{5,4},{6,5},{7,6},{8,7},{9,8},{10,9},{11,1... | collective-permute-start | bytes 49160 | tf_op jit(solution)/shard_map/ppermute | solution.py:24
  22.3 12.9 %copy-start.2 = (f32[4,32,1024]{2,1,0:T(8,128)S(1)}, f32[4,32,1024]{2,1,0:T(8,128)}, u32[]{:S(2)}) copy-start(f32[4,32,1024]{2,1,0:T(8,128)} %param.7) | copy-start | bytes 1572868
  22.7 12.6 %copy-start.1 = (s32[4,32,1024]{2,1,0:T(8,128)S(1)}, s32[4,32,1024]{2,1,0:T(8,128)}, u32[]{:S(2)}) copy-start(s32[4,32,1024]{2,1,0:T(8,128)} %param.6) | copy-start | bytes 1572868
  22.7 8.2 %copy-start.3 = (f32[16]{0:T(128)S(1)}, f32[16]{0:T(128)}, u32[]{:S(2)}) copy-start(f32[16]{0:T(128)} %param.9) | copy-start | bytes 196
  22.7 8.2 %copy-start.4 = (s32[8]{0:T(128)S(1)}, s32[8]{0:T(128)}, u32[]{:S(2)}) copy-start(s32[8]{0:T(128)} %param.8) | copy-start | bytes 100
  22.7 8.5 %collective-permute-start.4 = (f32[1,32,1024]{2,1,0:T(8,128)S(1)}, f32[1,32,1024]{2,1,0:T(8,128)S(1)}, u32[]{:S(2)}, u32[]{:S(2)}) collective-permute-start(f32[1,32,1024]{2,1,0:T(8,128)S(1)} %get-tuple-element.24), channel_id=1, source_target_pairs={{0,16},{16,32},{32,48},{48,64},{64,80},{80,96},{96,112},{112,128},... | collective-permute-start | bytes 393224 | tf_op jit(solution)/shard_map/ppermute | solution.py:22
  28.9 6.3 %collective-permute-start.5 = (f32[1,32,1024]{2,1,0:T(8,128)S(1)}, f32[1,32,1024]{2,1,0:T(8,128)S(1)}, u32[]{:S(2)}, u32[]{:S(2)}) collective-permute-start(f32[1,32,1024]{2,1,0:T(8,128)S(1)} %get-tuple-element.25), channel_id=1, source_target_pairs={{16,0},{32,16},{48,32},{64,48},{80,64},{96,80},{112,96},{128,112},... | collective-permute-start | bytes 393224 | tf_op jit(solution)/shard_map/ppermute | solution.py:24
  35.6 6.2 %collective-permute-start.7 = (f32[4,1,1024]{2,1,0:T(1,128)S(1)}, f32[4,1,1024]{2,1,0:T(1,128)S(1)}, u32[]{:S(2)}, u32[]{:S(2)}) collective-permute-start(f32[4,1,1024]{2,1,0:T(1,128)S(1)} %get-tuple-element.22), channel_id=1, source_target_pairs={{0,1},{1,2},{2,3},{3,4},{4,5},{5,6},{6,7},{7,8},{8,9},{9,10},{10,1... | collective-permute-start | bytes 49160 | tf_op jit(solution)/shard_map/ppermute | solution.py:22
  40.5 4.8 %collective-permute-start.6 = (f32[4,1,1024]{2,1,0:T(1,128)S(1)}, f32[4,1,1024]{2,1,0:T(1,128)S(1)}, u32[]{:S(2)}, u32[]{:S(2)}) collective-permute-start(f32[4,1,1024]{2,1,0:T(1,128)S(1)} %get-tuple-element.23), channel_id=1, source_target_pairs={{1,0},{2,1},{3,2},{4,3},{5,4},{6,5},{7,6},{8,7},{9,8},{10,9},{11,1... | collective-permute-start | bytes 49160 | tf_op jit(solution)/shard_map/ppermute | solution.py:24
  46.0 4.9 %collective-permute-start.9 = (f32[4,1,1024]{2,1,0:T(1,128)S(1)}, f32[4,1,1024]{2,1,0:T(1,128)S(1)}, u32[]{:S(2)}, u32[]{:S(2)}) collective-permute-start(f32[4,1,1024]{2,1,0:T(1,128)S(1)} %get-tuple-element.20), channel_id=1, source_target_pairs={{0,1},{1,2},{2,3},{3,4},{4,5},{5,6},{6,7},{7,8},{8,9},{9,10},{10,1... | collective-permute-start | bytes 49160 | tf_op jit(solution)/shard_map/ppermute | solution.py:22
  49.5 4.5 %collective-permute-start.8 = (f32[4,1,1024]{2,1,0:T(1,128)S(1)}, f32[4,1,1024]{2,1,0:T(1,128)S(1)}, u32[]{:S(2)}, u32[]{:S(2)}) collective-permute-start(f32[4,1,1024]{2,1,0:T(1,128)S(1)} %get-tuple-element.21), channel_id=1, source_target_pairs={{1,0},{2,1},{3,2},{4,3},{5,4},{6,5},{7,6},{8,7},{9,8},{10,9},{11,1... | collective-permute-start | bytes 49160 | tf_op jit(solution)/shard_map/ppermute | solution.py:24
  54.7 6.4 %collective-permute-start.10 = (f32[1,32,1024]{2,1,0:T(8,128)S(1)}, f32[1,32,1024]{2,1,0:T(8,128)S(1)}, u32[]{:S(2)}, u32[]{:S(2)}) collective-permute-start(f32[1,32,1024]{2,1,0:T(8,128)S(1)} %get-tuple-element.18), channel_id=1, source_target_pairs={{0,16},{16,32},{32,48},{48,64},{64,80},{80,96},{96,112},{112,128},... | collective-permute-start | bytes 393224 | tf_op jit(solution)/shard_map/ppermute | solution.py:22
  59.1 6.3 %collective-permute-start.11 = (f32[1,32,1024]{2,1,0:T(8,128)S(1)}, f32[1,32,1024]{2,1,0:T(8,128)S(1)}, u32[]{:S(2)}, u32[]{:S(2)}) collective-permute-start(f32[1,32,1024]{2,1,0:T(8,128)S(1)} %get-tuple-element.19), channel_id=1, source_target_pairs={{16,0},{32,16},{48,32},{64,48},{80,64},{96,80},{112,96},{128,112},... | collective-permute-start | bytes 393224 | tf_op jit(solution)/shard_map/ppermute | solution.py:24
  277.3 5.0 %collective-permute-start.13 = (f32[4,1,1024]{2,1,0:T(1,128)S(1)}, f32[4,1,1024]{2,1,0:T(1,128)S(1)}, u32[]{:S(2)}, u32[]{:S(2)}) collective-permute-start(f32[4,1,1024]{2,1,0:T(1,128)S(1)} %get-tuple-element.16), channel_id=1, source_target_pairs={{0,1},{1,2},{2,3},{3,4},{4,5},{5,6},{6,7},{7,8},{8,9},{9,10},{10,1... | collective-permute-start | bytes 49160 | tf_op jit(solution)/shard_map/ppermute | solution.py:22
  280.9 4.5 %collective-permute-start.12 = (f32[4,1,1024]{2,1,0:T(1,128)S(1)}, f32[4,1,1024]{2,1,0:T(1,128)S(1)}, u32[]{:S(2)}, u32[]{:S(2)}) collective-permute-start(f32[4,1,1024]{2,1,0:T(1,128)S(1)} %get-tuple-element.17), channel_id=1, source_target_pairs={{1,0},{2,1},{3,2},{4,3},{5,4},{6,5},{7,6},{8,7},{9,8},{10,9},{11,1... | collective-permute-start | bytes 49160 | tf_op jit(solution)/shard_map/ppermute | solution.py:24
  286.1 4.0 collective-permute-start.15
  288.8 4.5 %collective-permute-start.14 = (f32[4,1,1024]{2,1,0:T(1,128)S(1)}, f32[4,1,1024]{2,1,0:T(1,128)S(1)}, u32[]{:S(2)}, u32[]{:S(2)}) collective-permute-start(f32[4,1,1024]{2,1,0:T(1,128)S(1)} %get-tuple-element.15), channel_id=1, source_target_pairs={{1,0},{2,1},{3,2},{4,3},{5,4},{6,5},{7,6},{8,7},{9,8},{10,9},{11,1... | collective-permute-start | bytes 49160 | tf_op jit(solution)/shard_map/ppermute | solution.py:24
  294.0 8.0 %collective-permute-start.16 = (f32[1,32,1024]{2,1,0:T(8,128)S(1)}, f32[1,32,1024]{2,1,0:T(8,128)S(1)}, u32[]{:S(2)}, u32[]{:S(2)}) collective-permute-start(f32[1,32,1024]{2,1,0:T(8,128)S(1)} %get-tuple-element.12), channel_id=1, source_target_pairs={{0,16},{16,32},{32,48},{48,64},{64,80},{80,96},{96,112},{112,128},... | collective-permute-start | bytes 393224 | tf_op jit(solution)/shard_map/ppermute | solution.py:22
  300.1 6.3 %collective-permute-start.17 = (f32[1,32,1024]{2,1,0:T(8,128)S(1)}, f32[1,32,1024]{2,1,0:T(8,128)S(1)}, u32[]{:S(2)}, u32[]{:S(2)}) collective-permute-start(f32[1,32,1024]{2,1,0:T(8,128)S(1)} %get-tuple-element.13), channel_id=1, source_target_pairs={{16,0},{32,16},{48,32},{64,48},{80,64},{96,80},{112,96},{128,112},... | collective-permute-start | bytes 393224 | tf_op jit(solution)/shard_map/ppermute | solution.py:24
where the time goes:
time: 415 us; the launch traced here: 414 us
  blocking collectives  311 us (75%)
  starting transfers between devices  53.4 us (13%)
  waiting for transfers between devices  33.3 us (8%)
  other arithmetic  9.68 us (2%)
  between operations  5.07 us (1%)
    psum x2, blocking collectives, squares(): return lax.psum(jnp.sum(residual * residual), ('tm', 'space'))  207 us
    psum x1, blocking collectives, body(): curvature = lax.psum(jnp.sum(direction * image_vec), ('tm', 'space'))  104 us
    ppermute x9, starting transfers between devices, padded_2(): lax.ppermute(tail, axis, [(i, (i + 1) % count) for i in range(ends)])  39.7 us
    ppermute x9, waiting for transfers between devices, padded_2(): lax.ppermute(head, axis, [((i + 1) % count, i) for i in range(ends)])  33.3 us
    ppermute x9, starting transfers between devices, padded_2(): lax.ppermute(head, axis, [((i + 1) % count, i) for i in range(ends)])  13.6 us
  transfers between devices with their start and end apart: 18, of which 9 were waited for; matrix products, arithmetic and copies ran while one was open for 0% of the time, Pallas kernels for 0%

commit v1 on v0

v1 whole, which is shorter than its diff:
```python
import jax
import jax.numpy as jnp
from jax import lax
from jax.sharding import PartitionSpec as P

kappa_square = 0.3
time_corr = 0.9
prior_scale = 0.05

COUPLE = prior_scale * time_corr
INNER = prior_scale * (1.0 + time_corr * time_corr)


def exchange(up_edge, down_edge, axis):
    count = lax.axis_size(axis)
    before = lax.ppermute(down_edge, axis, [(i, i + 1) for i in range(count - 1)])
    after = lax.ppermute(up_edge, axis, [(i + 1, i) for i in range(count - 1)])
    return before, after


def grid_rows(rows, halo, own):
    row = lax.axis_index("space") * own - halo + jnp.arange(rows)
    total = own * lax.axis_size("space")
    return ((row >= 0) & (row < total)).astype(jnp.float32)[None, :, None]


def stiffness_rows(field):
    padded = jnp.pad(field[:, 1:-1, :], ((0, 0), (0, 0), (1, 1)))
    neighbours = field[:, 2:, :] + field[:, :-2, :] + padded[:, :, 2:] + padded[:, :, :-2]
    return (kappa_square + 4.0) * field[:, 1:-1, :] - neighbours


def smooth(field, halo, own):
    once = stiffness_rows(field)
    once = once * grid_rows(once.shape[1], halo - 1, own)
    twice = stiffness_rows(once)
    if halo > 2:
        twice = twice * grid_rows(twice.shape[1], halo - 2, own)
    return twice


def recentre(sets, axis):
    count = lax.axis_size(axis)
    got = lax.all_to_all(jnp.broadcast_to(sets[None], (count,) + sets.shape), axis, 0, 0)
    uu, uw, ww, uy, wy, ratio = (got[:, k] for k in range(6))
    total = jnp.sum(uu, axis=0)
    centre = jnp.sum(uw + ratio * uu, axis=0) / total
    centre = jnp.where(total > 0, centre, 0.0)
    e = ratio - centre[None]
    ec = e * ratio
    uw_new = uw + e * uu
    ww_new = ww + e * (2.0 * uw + e * uu)
    uy_new = uy + e * uw + ec * uu
    wy_new = wy + e * (ww + ratio * uw + uy) + e * e * (uw + ratio * uu)
    parts = [total] + [jnp.sum(v, axis=0) for v in (uw_new, ww_new, uy_new, wy_new)] + [centre]
    return jnp.stack(parts + [jnp.zeros_like(total)] * 2)


def body(latent, counts, exposure, region_ids, coefficients):
    days, own, columns = latent.shape
    blocks = region_ids.shape[0]
    one_hot = (region_ids[:, None] == jnp.arange(coefficients.shape[0])[None, :]).astype(
        jnp.float32
    )
    block_offset = jnp.sum(one_hot * coefficients[None, :], axis=1)
    offset = jnp.broadcast_to(block_offset[:, None], (blocks, own // blocks)).reshape(own)
    intensity = exposure * jnp.exp(offset[None, :, None] + latent)
    excess = intensity - counts.astype(jnp.float32)

    def packed(lo):
        pieces = []
        for field, width in ((latent, 6), (excess, 4), (intensity, 2)):
            rows = field[:, :width] if lo else field[:, own - width :]
            pieces.append(rows.reshape(days * width, columns))
        return jnp.concatenate(pieces)

    above, below = exchange(packed(True), packed(False), "space")

    def unpacked(message):
        cut = (days * 6, days * 10)
        return (
            message[: cut[0]].reshape(days, 6, columns),
            message[cut[0] : cut[1]].reshape(days, 4, columns),
            message[cut[1] :].reshape(days, 2, columns),
        )

    latent6, excess4, intensity2 = (
        jnp.concatenate([a, field, b], axis=1)
        for a, field, b in zip(unpacked(above), (latent, excess, intensity), unpacked(below))
    )

    tm_at, tm_count = lax.axis_index("tm"), lax.axis_size("tm")
    has_before = (tm_at > 0).astype(jnp.float32)
    has_after = (tm_at < tm_count - 1).astype(jnp.float32)
    first = jnp.where(tm_at == 0, prior_scale, INNER).astype(jnp.float32)
    last = jnp.where(tm_at == tm_count - 1, prior_scale, INNER).astype(jnp.float32)
    weight = [first] + [jnp.float32(INNER)] * (days - 2) + [last]

    spatial = smooth(latent6, 6, own)
    on4 = grid_rows(own + 8, 4, own)[0]
    residual = []
    for t in range(days):
        value = weight[t] * spatial[t] + excess4[t]
        if t > 0:
            value = value - COUPLE * spatial[t - 1]
        if t < days - 1:
            value = value - COUPLE * spatial[t + 1]
        residual.append(-value * on4)
    inner = smooth(jnp.stack(residual[1:-1]), 4, own)
    to_before = jnp.concatenate([spatial[0], residual[0], -COUPLE * inner[0], intensity2[0]])
    to_after = jnp.concatenate([spatial[-1], residual[-1], -COUPLE * inner[-1], intensity2[-1]])
    from_before, from_after = exchange(to_before, to_after, "tm")

    def parts(message):
        a, b, c = own + 8, 2 * own + 16, 3 * own + 20
        return message[:a], message[a:b], message[b:c], message[c:]

    s_b, r_b, q_b, i_b = parts(from_before)
    s_a, r_a, q_a, i_a = parts(from_after)
    r_b = (r_b + COUPLE * spatial[0]) * has_before
    r_a = (r_a + COUPLE * spatial[-1]) * has_after
    residual[0] = residual[0] + COUPLE * s_b
    residual[-1] = residual[-1] + COUPLE * s_a
    outer = smooth(jnp.stack([r_b, residual[0], residual[-1], r_a]), 4, own)
    filtered = [outer[0], outer[1]] + [inner[k] for k in range(days - 2)] + [outer[2], outer[3]]
    mid = slice(2, -2)
    image = []
    for t in range(days):
        image.append(
            weight[t] * filtered[t + 1]
            - COUPLE * (filtered[t] + filtered[t + 2])
            + intensity2[t] * residual[t][mid]
        )
    image_b = (INNER * filtered[0] - COUPLE * filtered[1] + q_b + i_b * r_b[mid]) * has_before
    image_a = (INNER * filtered[-1] - COUPLE * filtered[-2] + q_a + i_a * r_a[mid]) * has_after
    twice = smooth(jnp.stack([image_b] + image + [image_a]), 2, own)
    u = jnp.stack([value[4:-4] for value in residual])
    q = jnp.stack([value[mid] for value in image])
    z = jnp.stack(
        [
            weight[t] * twice[t + 1]
            - COUPLE * (twice[t] + twice[t + 2])
            + intensity[t] * q[t]
            for t in range(days)
        ]
    )

    uu, uq = jnp.sum(u * u), jnp.sum(u * q)
    ratio = jnp.where(uu > 0, uq / uu, 0.0)
    w = q - ratio * u
    y = z - ratio * q
    moments = jnp.stack(
        [uu, jnp.sum(u * w), jnp.sum(w * w), jnp.sum(u * y), jnp.sum(w * y), ratio, uu, uu]
    )
    sets = jnp.broadcast_to(moments[:, None], (8, 128))
    sets = recentre(recentre(sets, "tm"), "space")
    m0, ww, wy, centre = sets[0, 0], sets[2, 0], sets[4, 0], sets[5, 0]
    alpha0 = 1.0 / centre
    norm1 = alpha0 * alpha0 * ww
    beta = norm1 / m0
    curvature1 = alpha0 * alpha0 * wy - beta * beta * (centre * m0)
    alpha1 = norm1 / curvature1
    residual1 = u - alpha0 * q
    direction1 = residual1 + beta * u
    image1 = (q - alpha0 * z) + beta * q
    return (latent + (alpha0 * u + alpha1 * direction1), residual1 - alpha1 * image1)


def solution(mesh):
    return jax.shard_map(
        body,
        mesh=mesh,
        in_specs=(
            P("tm", "space", None),
            P("tm", "space", None),
            P("tm", "space", None),
            P("space"),
            P(),
        ),
        out_specs=(P("tm", "space", None), P("tm", "space", None)),
        check_vma=False,
    )
```

time: 415 us -> 111 us (0.27)
  blocking collectives: 311 us -> 41.9 us
  starting transfers between devices: 53.4 us -> 13.6 us
  waiting for transfers between devices: 33.3 us -> 22.9 us
  other arithmetic: 9.68 us -> 19.5 us
  local copies, waits for them, and re-layouts: 1.37 us -> 8.57 us
    psum x3 -> x0, blocking collectives: 311 us -> none  [the longest x2 207 us: squares(): return lax.psum(jnp.sum(residual * residual), ('tm', 'space'))]
    all_to_all x0 -> x2, blocking collectives: none -> 41.9 us  [recentre(): lax.all_to_all(jnp.broadcast_to(sets[None], (count,) + sets.shape), axis,...]
    ppermute x18 -> x4, starting transfers between devices: 53.4 us -> 13.6 us  [the longest x2 10.4 us: exchange(): lax.ppermute(down_edge, axis, [(i, i + 1) for i in range(count - 1)])]
    ppermute x18 -> x4, waiting for transfers between devices: 33.3 us -> 22.9 us  [the longest x2 14.4 us: exchange(): after = lax.ppermute(up_edge, axis, [(i + 1, i) for i in range(count - 1)])]
    mul x0 -> x10, other arithmetic: none -> 6.16 us  [the longest x3 2.68 us: smooth(): twice = twice * grid_rows(twice.shape[1], halo - 2, own)]
    another operation x0 -> x8, local copies, waits for them, and re-layouts: none -> 4.69 us  [the longest x1 4.53 us: body(): jnp.stack([uu, jnp.sum(u * w), jnp.sum(w * w), jnp.sum(u * y), jnp.sum(w...]
  transfers between devices with their start and end apart: 18 -> 4, of which waited for: 9 -> 4; matrix products, arithmetic and copies ran while one was open for 0% -> 0% of each run, Pallas kernels for 0% -> 0%
where the time goes in v1:
time: 111 us; the launch traced here: 110 us
  blocking collectives  41.9 us (38%)
  waiting for transfers between devices  22.9 us (21%)
  other arithmetic  19.5 us (18%)
  starting transfers between devices  13.6 us (12%)
  local copies, waits for them, and re-layouts  8.57 us (8%)
  between operations  3.56 us (3%)
    all_to_all x2, blocking collectives, recentre(): lax.all_to_all(jnp.broadcast_to(sets[None], (count,) + sets.shape), axis,...  41.9 us
    ppermute x2, waiting for transfers between devices, exchange(): after = lax.ppermute(up_edge, axis, [(i + 1, i) for i in range(count - 1)])  14.4 us
    ppermute x2, starting transfers between devices, exchange(): lax.ppermute(down_edge, axis, [(i, i + 1) for i in range(count - 1)])  10.4 us
    ppermute x2, waiting for transfers between devices, exchange(): lax.ppermute(down_edge, axis, [(i, i + 1) for i in range(count - 1)])  8.54 us
    another operation x1, local copies, waits for them, and re-layouts, body(): jnp.stack([uu, jnp.sum(u * w), jnp.sum(w * w), jnp.sum(u * y), jnp.sum(w...  4.53 us
    ppermute x2, starting transfers between devices, exchange(): after = lax.ppermute(up_edge, axis, [(i + 1, i) for i in range(count - 1)])  3.21 us
    mul x3, other arithmetic, smooth(): twice = twice * grid_rows(twice.shape[1], halo - 2, own)  2.68 us
  transfers between devices with their start and end apart: 4, of which 4 were waited for; matrix products, arithmetic and copies ran while one was open for 0% of the time, Pallas kernels for 0%

profile of v1, /device:TPU:1, one launch (start us, length us, event | category | flops | bytes accessed | tf_op | source)
XLA Modules:
  0.0 110.0 jit_solution(17687753623731896701)
XLA Ops:
  0.6 0.9 select_reduce_fusion
  1.6 0.1 add.328
  1.6 1.0 fusion.99
  2.6 1.6 %convert_subtract_fusion = (f32[4,32,1024]{2,1,0:T(8,128)S(1)}, f32[4,32,1024]{2,1,0:T(8,128)S(1)}) fusion(s32[4,32,1024]{2,1,0:T(8,128)} %param.6, f32[4,32,1024]{2,1,0:T(8,128)} %param.7, f32[4,32,1024]{2,1,0:T(8,128)} %param.5, f32[32]{0:T(128)S(1)} %add.328), kind=kLoop, calls=%fused_computation.61 | loop fusion | flops 524288 | bytes 2621568 | tf_op jit(solution)/shard_map/sub | solution.py:68
  4.4 4.5 %collective-permute-start = (f32[48,1024]{1,0:T(8,128)S(1)}, f32[48,1024]{1,0:T(8,128)S(1)}, u32[]{:S(2)}, u32[]{:S(2)}) collective-permute-start(f32[48,1024]{1,0:T(8,128)S(1)} %pad_maximum_fusion.10), channel_id=1, source_target_pairs={{0,1},{1,2},{2,3},{3,4},{4,5},{5,6},{6,7},{7,8},{8,9},{9,10},{10,1... | collective-permute-start | bytes 589832 | tf_op jit(solution)/shard_map/ppermute | solution.py:16
  9.0 1.3 %collective-permute-start.1 = (f32[48,1024]{1,0:T(8,128)S(1)}, f32[48,1024]{1,0:T(8,128)S(1)}, u32[]{:S(2)}, u32[]{:S(2)}) collective-permute-start(f32[48,1024]{1,0:T(8,128)S(1)} %pad_maximum_fusion.11), channel_id=1, source_target_pairs={{1,0},{2,1},{3,2},{4,3},{5,4},{6,5},{7,6},{8,7},{9,8},{10,9},{11,1... | collective-permute-start | bytes 589832 | tf_op jit(solution)/shard_map/ppermute | solution.py:17
  10.4 1.1 collective-permute-done
  11.5 4.1 %collective-permute-done.1 = f32[48,1024]{1,0:T(8,128)S(1)} collective-permute-done((f32[48,1024]{1,0:T(8,128)S(1)}, f32[48,1024]{1,0:T(8,128)S(1)}, u32[]{:S(2)}, u32[]{:S(2)}) %collective-permute-start.1) | collective-permute-done | bytes 196640 | tf_op jit(solution)/shard_map/ppermute | solution.py:17
  15.7 0.1 pad_maximum_fusion
  15.8 0.1 slice.506
  15.9 0.5 fusion.7
  16.4 0.9 slice.509
  17.4 2.0 %fusion.14 = (f32[4,40,1024]{2,1,0:T(8,128)S(1)}, f32[4,40,1024]{2,1,0:T(8,128)S(1)}) fusion(f32[4,40,1024]{2,1,0:T(8,128)} %slice.509, f32[4,42,1024]{2,1,0:T(8,128)S(1)} %fusion.7, f32[40]{0:T(128)S(1)} %and_convert_fusion.3, f32[4,4,1024]{2,1,0:T(4,128)S(1)} %reshape.222, f32[4,32,1024]{2,1,0:T(8,128)S(1)} %get-tuple-element.22, ...), kind=kLoop, calls=%fused_computation.30 | loop fusion | flops 1310720 | bytes 3932320 | tf_op jit(solution)/shard_map/mul | solution.py:38
  19.4 0.8 negate_multiply_fusion
  20.2 0.1 fusion.60
  20.4 0.2 fusion.26
  20.8 0.2 fusion.30
  21.0 0.8 multiply_bitcast_fusion
  21.9 0.1 pad_maximum_fusion.2
  21.9 0.7 slice_bitcast_fusion.2
  22.6 0.1 copy-done.4
  22.8 0.1 copy-done.5
  22.8 0.9 pad_maximum_fusion.4
  23.8 5.9 %collective-permute-start.2 = (f32[152,1024]{1,0:T(8,128)}, f32[152,1024]{1,0:T(8,128)}, u32[]{:S(2)}, u32[]{:S(2)}) collective-permute-start(f32[152,1024]{1,0:T(8,128)} %pad_maximum_fusion.4), channel_id=1, source_target_pairs={{0,16},{16,32},{32,48},{48,64},{64,80},{80,96},{96,112},{112,128},... | collective-permute-start | bytes 1867784 | tf_op jit(solution)/shard_map/ppermute | solution.py:16
  29.7 7.4 %collective-permute-done.2 = f32[152,1024]{1,0:T(8,128)} collective-permute-done((f32[152,1024]{1,0:T(8,128)}, f32[152,1024]{1,0:T(8,128)}, u32[]{:S(2)}, u32[]{:S(2)}) %collective-permute-start.2) | collective-permute-done | bytes 622624 | tf_op jit(solution)/shard_map/ppermute | solution.py:16
  37.1 1.2 %fusion.49 = (f32[40,1024]{1,0:T(8,128)S(1)}, f32[40,1024]{1,0:T(8,128)S(1)}, f32[40,1024]{1,0:T(8,128)S(1)}) fusion(f32[152,1024]{1,0:T(8,128)} %collective-permute-done.2, f32[40]{0:T(128)S(1)} %and_convert_fusion.3, f32[4,40,1024]{2,1,0:T(8,128)S(1)} %get-tuple-element.64, f32[4,40,1024]{2,1,0:T(8,128)} %copy-done.1, f32[]{:T(128)S(6)} %select_n.38, ...), kind=kLoop, calls=%fused_computation.116 | loop fusion | flops 450560 | bytes 1310888 | tf_op jit(solution)/shard_map/add | solution.py:122
  38.3 1.1 pad_maximum_fusion.5
  39.3 1.9 %collective-permute-start.3 = (f32[152,1024]{1,0:T(8,128)S(1)}, f32[152,1024]{1,0:T(8,128)S(1)}, u32[]{:S(2)}, u32[]{:S(2)}) collective-permute-start(f32[152,1024]{1,0:T(8,128)S(1)} %pad_maximum_fusion.5), channel_id=1, source_target_pairs={{16,0},{32,16},{48,32},{64,48},{80,64},{96,80},{112,96},{128,112},... | collective-permute-start | bytes 1867784 | tf_op jit(solution)/shard_map/ppermute | solution.py:17
  41.3 10.3 %collective-permute-done.3 = f32[152,1024]{1,0:T(8,128)S(1)} collective-permute-done((f32[152,1024]{1,0:T(8,128)S(1)}, f32[152,1024]{1,0:T(8,128)S(1)}, u32[]{:S(2)}, u32[]{:S(2)}) %collective-permute-start.3) | collective-permute-done | bytes 622624 | tf_op jit(solution)/shard_map/ppermute | solution.py:17
  51.9 0.4 fusion.18
  52.4 0.4 fusion.22
  52.8 1.1 %fusion.41 = f32[6,36,1024]{2,1,0:T(8,128)S(1)} fusion(f32[40,1024]{1,0:T(8,128)S(1)} %get-tuple-element.32, f32[152,1024]{1,0:T(8,128)} %collective-permute-done.2, f32[4,36,1024]{2,1,0:T(8,128)S(1)} %fusion.22, f32[]{:T(128)S(6)} %convert_element_type.73), kind=kLoop, calls=%fused_computation.96 | loop fusion | flops 258047 | bytes 901124
  54.1 0.1 bitcast_dynamic-update-slice_fusion
  54.3 0.1 slice.569
  54.4 0.6 fusion.3
  55.0 0.1 slice.572
  55.1 0.5 fusion.10
  55.6 0.1 fusion.78
  55.8 0.8 multiply_reduce_fusion.4
  58.5 0.8 multiply_reduce_fusion
  59.4 0.8 multiply_reduce_fusion.1
  60.1 0.8 multiply_reduce_fusion.2
  61.0 4.5 %stack.173 = f32[8]{0:T(128)S(1)} concatenate(f32[1]{0:T(128)} %bitcast.16, f32[1]{0:T(128)} %bitcast.31, f32[1]{0:T(128)} %bitcast.32, f32[1]{0:T(128)} %bitcast.53, f32[1]{0:T(128)} %bitcast.54, f32[1]{0:T(128)} %bitcast.55, f32[1]{0:T(128)} %bitcast.16, f32[1]{0:T(128)} %bitcast.16), dimensions={0} | concatenate | bytes 64 | tf_op jit(solution)/shard_map/stack | solution.py:152
  65.5 0.1 broadcast_in_dim_broadcast_in_dim_broadcast_in_dim.2
  65.6 15.9 %all_to_all.10 = f32[32,8,128]{2,1,0:T(8,128)S(1)} all-to-all(f32[32,8,128]{2,1,0:T(8,128)S(1)} %broadcast_in_dim_broadcast_in_dim_broadcast_in_dim.2), channel_id=1, replica_groups=mesh['tm'=32,'space'=16] {'tm'}, dimensions={0} | all-to-all | bytes 262144 | tf_op jit(solution)/shard_map/all_to_all | solution.py:44
  81.7 26.0 %all_to_all.11 = f32[16,8,128]{2,1,0:T(8,128)S(1)} all-to-all(f32[16,8,128]{2,1,0:T(8,128)S(1)} %broadcast_in_dim.7), channel_id=1, replica_groups=mesh['tm'=32,'space'=16] {'space'}, dimensions={0} | all-to-all | bytes 131072 | tf_op jit(solution)/shard_map/all_to_all | solution.py:44
  108.1 0.9 multiply_subtract_fusion
  109.1 0.9 add_add_fusion
  (74 shorter events, 1.5 us)
Async XLA Ops:
  4.4 11.3 %copy-start = (f32[4,32,1024]{2,1,0:T(8,128)S(1)}, f32[4,32,1024]{2,1,0:T(8,128)}, u32[]{:S(2)}) copy-start(f32[4,32,1024]{2,1,0:T(8,128)} %param.5) | copy-start | bytes 1572868
  4.4 7.1 %collective-permute-start = (f32[48,1024]{1,0:T(8,128)S(1)}, f32[48,1024]{1,0:T(8,128)S(1)}, u32[]{:S(2)}, u32[]{:S(2)}) collective-permute-start(f32[48,1024]{1,0:T(8,128)S(1)} %pad_maximum_fusion.10), channel_id=1, source_target_pairs={{0,1},{1,2},{2,3},{3,4},{4,5},{5,6},{6,7},{7,8},{8,9},{9,10},{10,1... | collective-permute-start | bytes 589832 | tf_op jit(solution)/shard_map/ppermute | solution.py:16
  9.0 6.6 %collective-permute-start.1 = (f32[48,1024]{1,0:T(8,128)S(1)}, f32[48,1024]{1,0:T(8,128)S(1)}, u32[]{:S(2)}, u32[]{:S(2)}) collective-permute-start(f32[48,1024]{1,0:T(8,128)S(1)} %pad_maximum_fusion.11), channel_id=1, source_target_pairs={{1,0},{2,1},{3,2},{4,3},{5,4},{6,5},{7,6},{8,7},{9,8},{10,9},{11,1... | collective-permute-start | bytes 589832 | tf_op jit(solution)/shard_map/ppermute | solution.py:17
  11.5 5.8 %copy-start.6 = (f32[48,1024]{1,0:T(8,128)}, f32[48,1024]{1,0:T(8,128)S(1)}, u32[]{:S(2)}) copy-start(f32[48,1024]{1,0:T(8,128)S(1)} %collective-permute-done) | copy-start | bytes 589828
  15.6 1.7 %copy-start.7 = (f32[48,1024]{1,0:T(8,128)}, f32[48,1024]{1,0:T(8,128)S(1)}, u32[]{:S(2)}) copy-start(f32[48,1024]{1,0:T(8,128)S(1)} %collective-permute-done.1) | copy-start | bytes 589828
  19.4 1.0 copy-start.1
  20.4 20.9 %copy-start.2 = (f32[40,1024]{1,0:T(8,128)}, f32[40,1024]{1,0:T(8,128)S(1)}, u32[]{:S(2)}) copy-start(f32[40,1024]{1,0:T(8,128)S(1)} %get-tuple-element.25) | copy-start | bytes 491524
  20.7 1.0 slice-start
  20.7 1.1 slice-start.1
  21.8 0.9 copy-start.4
  21.8 1.0 copy-start.5
  23.8 13.4 %collective-permute-start.2 = (f32[152,1024]{1,0:T(8,128)}, f32[152,1024]{1,0:T(8,128)}, u32[]{:S(2)}, u32[]{:S(2)}) collective-permute-start(f32[152,1024]{1,0:T(8,128)} %pad_maximum_fusion.4), channel_id=1, source_target_pairs={{0,16},{16,32},{32,48},{48,64},{64,80},{80,96},{96,112},{112,128},... | collective-permute-start | bytes 1867784 | tf_op jit(solution)/shard_map/ppermute | solution.py:16
  39.3 12.3 %collective-permute-start.3 = (f32[152,1024]{1,0:T(8,128)S(1)}, f32[152,1024]{1,0:T(8,128)S(1)}, u32[]{:S(2)}, u32[]{:S(2)}) collective-permute-start(f32[152,1024]{1,0:T(8,128)S(1)} %pad_maximum_fusion.5), channel_id=1, source_target_pairs={{16,0},{32,16},{48,32},{64,48},{80,64},{96,80},{112,96},{128,112},... | collective-permute-start | bytes 1867784 | tf_op jit(solution)/shard_map/ppermute | solution.py:17
  52.8 1.2 %copy-start.3 = (f32[40,1024]{1,0:T(8,128)S(1)}, f32[40,1024]{1,0:T(8,128)}, u32[]{:S(2)}) copy-start(f32[40,1024]{1,0:T(8,128)} %copy-done.2) | copy-start | bytes 491524

commit v2 on v0

v2 whole, which is shorter than its diff:
```python
import functools

import jax
import jax.numpy as jnp
from jax import lax
from jax.experimental import pallas as pl
from jax.experimental.pallas import tpu as pltpu
from jax.sharding import PartitionSpec as P

kappa_square = 0.3
time_corr = 0.9
prior_scale = 0.05

COUPLE = prior_scale * time_corr
INNER = prior_scale * (1.0 + time_corr * time_corr)
DIAG = kappa_square + 4.0

DAYS, OWN, COLUMNS = 4, 32, 1024
PAD = 8
FRAME = OWN + 2 * PAD
TILES = FRAME // 8
REGION_ROWS = 4
WIDE, SLIM = OWN + 8, OWN + 4
MESSAGE = 2 * WIDE + 2 * SLIM
EDGE = DAYS * 12

VMEM = pl.BlockSpec(memory_space=pltpu.VMEM)
SMEM = pl.BlockSpec(memory_space=pltpu.SMEM)
PARAMS = pltpu.CompilerParams(vmem_limit_bytes=40 * 1024 * 1024)


def f32(*shape):
    return jax.ShapeDtypeStruct(shape, jnp.float32)


def row_iota():
    return lax.broadcasted_iota(jnp.int32, (8, COLUMNS), 0)


def column_iota():
    return lax.broadcasted_iota(jnp.int32, (8, COLUMNS), 1)


def tile(i):
    return pl.ds(pl.multiple_of(i * 8, 8), 8)


def on_grid(at_ref, i):
    sp, count = at_ref[0], at_ref[2]
    off = ((i == 0) & (sp == 0)) | ((i == TILES - 1) & (sp == count - 1))
    return jnp.logical_not(off)


def apply_k(at_ref, src, dst, planes):
    row, column = row_iota(), column_iota()

    def step(i, carry):
        keep = on_grid(at_ref, i)
        for s, d in planes:
            cur = src[s, tile(i), :]
            prev = src[s, tile(jnp.maximum(i - 1, 0)), :]
            nxt = src[s, tile(jnp.minimum(i + 1, TILES - 1)), :]
            up = pltpu.roll(jnp.where(row == 7, prev, cur), 1, 0)
            down = pltpu.roll(jnp.where(row == 0, nxt, cur), 7, 0)
            left = jnp.where(column == 0, 0.0, pltpu.roll(cur, 1, 1))
            right = jnp.where(column == COLUMNS - 1, 0.0, pltpu.roll(cur, COLUMNS - 1, 1))
            out = DIAG * cur - ((up + down) + (left + right))
            dst[d, tile(i), :] = jnp.where(keep, out, 0.0)
        return carry

    lax.fori_loop(0, TILES, step, 0)


def day_weights(at_ref):
    tm, count = at_ref[1], at_ref[3]
    first = jnp.where(tm == 0, prior_scale, INNER).astype(jnp.float32)
    last = jnp.where(tm == count - 1, prior_scale, INNER).astype(jnp.float32)
    return [first] + [jnp.float32(INNER)] * (DAYS - 2) + [last]


def intensity_kernel(ids, coef, latent, counts, exposure, intensity, excess, head, tail):
    row = row_iota()
    for i in range(OWN // 8):
        rows = slice(8 * i, 8 * i + 8)
        offset = jnp.where(row < REGION_ROWS, coef[ids[2 * i]], coef[ids[2 * i + 1]])
        for t in range(DAYS):
            value = exposure[t, rows, :] * jnp.exp(offset + latent[t, rows, :])
            intensity[t, rows, :] = value
            excess[t, rows, :] = value - counts[t, rows, :].astype(jnp.float32)
    start = 0
    for field, width in ((latent, 6), (excess, 4), (intensity, 2)):
        for t in range(DAYS):
            head[start : start + width, :] = field[t, :width, :]
            tail[start : start + width, :] = field[t, OWN - width :, :]
            start += width


def residual_kernel(
    at, latent, excess, intensity, above, below, res, inten, ends, inner, y_msg, c_msg, lat, exc, tmp
):
    start = 0
    for field, frame, width in ((latent, lat, 6), (excess, exc, 4), (intensity, inten, 2)):
        for t in range(DAYS):
            frame[t, PAD : PAD + OWN, :] = field[t]
            frame[t, PAD - width : PAD, :] = above[start : start + width, :]
            frame[t, PAD + OWN : PAD + OWN + width, :] = below[start : start + width, :]
            start += width
    same = [(t, t) for t in range(DAYS)]
    apply_k(at, lat, tmp, same)
    apply_k(at, tmp, lat, same)
    weight = day_weights(at)

    def combine(i, carry):
        s = [lat[t, tile(i), :] for t in range(DAYS)]
        for t in range(DAYS):
            value = weight[t] * s[t] + exc[t, tile(i), :]
            if t > 0:
                value = value - COUPLE * s[t - 1]
            if t < DAYS - 1:
                value = value - COUPLE * s[t + 1]
            res[t, tile(i), :] = -value
        ends[0, tile(i), :] = s[0]
        ends[1, tile(i), :] = s[DAYS - 1]
        return carry

    lax.fori_loop(0, TILES, combine, 0)
    middle = list(range(DAYS - 2))
    apply_k(at, res, tmp, [(k + 1, k) for k in middle])
    apply_k(at, tmp, inner, [(k, k) for k in middle])

    def pack(msg, day, nearest):
        msg[:WIDE, :] = lat[day, PAD - 4 : PAD + OWN + 4, :]
        msg[WIDE : 2 * WIDE, :] = res[day, PAD - 4 : PAD + OWN + 4, :]
        msg[2 * WIDE : 2 * WIDE + SLIM, :] = -COUPLE * inner[nearest, PAD - 2 : PAD + OWN + 2, :]
        msg[2 * WIDE + SLIM :, :] = inten[day, PAD - 2 : PAD + OWN + 2, :]

    even = lax.rem(at[1], 2) == 0

    @pl.when(even)
    def _():
        pack(y_msg, 0, 0)
        pack(c_msg, DAYS - 1, DAYS - 3)

    @pl.when(jnp.logical_not(even))
    def _():
        pack(c_msg, 0, 0)
        pack(y_msg, DAYS - 1, DAYS - 3)


def image_kernel(
    at, res, inten, ends, inner, intensity, y_msg, c_msg, u_out, q_out, z_out, sets, r6, f6, q6, tmp, got
):
    even = lax.rem(at[1], 2) == 0

    def unpack(msg, side):
        got[side, PAD - 4 : PAD + OWN + 4, :] = msg[:WIDE, :]
        got[2 + side, PAD - 4 : PAD + OWN + 4, :] = msg[WIDE : 2 * WIDE, :]
        got[4 + side, PAD - 2 : PAD + OWN + 2, :] = msg[2 * WIDE : 2 * WIDE + SLIM, :]
        got[6 + side, PAD - 2 : PAD + OWN + 2, :] = msg[2 * WIDE + SLIM :, :]

    @pl.when(even)
    def _():
        unpack(y_msg, 0)
        unpack(c_msg, 1)

    @pl.when(jnp.logical_not(even))
    def _():
        unpack(c_msg, 0)
        unpack(y_msg, 1)

    has = (at[1] > 0, at[1] < at[3] - 1)
    weight = day_weights(at)
    last = DAYS + 1

    def finish(i, carry):
        r6[0, tile(i), :] = jnp.where(has[0], got[2, tile(i), :] + COUPLE * ends[0, tile(i), :], 0.0)
        r6[last, tile(i), :] = jnp.where(has[1], got[3, tile(i), :] + COUPLE * ends[1, tile(i), :], 0.0)
        r6[1, tile(i), :] = res[0, tile(i), :] + COUPLE * got[0, tile(i), :]
        r6[DAYS, tile(i), :] = res[DAYS - 1, tile(i), :] + COUPLE * got[1, tile(i), :]
        for t in range(1, DAYS - 1):
            r6[t + 1, tile(i), :] = res[t, tile(i), :]
            f6[t + 1, tile(i), :] = inner[t - 1, tile(i), :]
        return carry

    lax.fori_loop(0, TILES, finish, 0)
    outer = [(0, 0), (1, 1), (DAYS, DAYS), (last, last)]
    apply_k(at, r6, tmp, outer)
    apply_k(at, tmp, f6, outer)

    def image(i, carry):
        f = [f6[t, tile(i), :] for t in range(DAYS + 2)]
        r = [r6[t, tile(i), :] for t in range(DAYS + 2)]
        for t in range(DAYS):
            q6[t + 1, tile(i), :] = (
                weight[t] * f[t + 1] - COUPLE * (f[t] + f[t + 2]) + inten[t, tile(i), :] * r[t + 1]
            )
        before = INNER * f[0] - COUPLE * f[1] + got[4, tile(i), :] + got[6, tile(i), :] * r[0]
        after = INNER * f[last] - COUPLE * f[DAYS] + got[5, tile(i), :] + got[7, tile(i), :] * r[last]
        q6[0, tile(i), :] = jnp.where(has[0], before, 0.0)
        q6[last, tile(i), :] = jnp.where(has[1], after, 0.0)
        return carry

    lax.fori_loop(0, TILES, image, 0)
    every = [(t, t) for t in range(DAYS + 2)]
    apply_k(at, q6, tmp, every)
    apply_k(at, tmp, f6, every)
    zero = jnp.zeros((8, COLUMNS), jnp.float32)

    def product(i, carry):
        uu, uq = carry
        k = i + PAD // 8
        f = [f6[t, tile(k), :] for t in range(DAYS + 2)]
        for t in range(DAYS):
            q, u = q6[t + 1, tile(k), :], r6[t + 1, tile(k), :]
            z = weight[t] * f[t + 1] - COUPLE * (f[t] + f[t + 2]) + intensity[t, tile(i), :] * q
            z_out[t, tile(i), :] = z
            q_out[t, tile(i), :] = q
            u_out[t, tile(i), :] = u
            uu = uu + u * u
            uq = uq + u * q
        return uu, uq

    uu, uq = lax.fori_loop(0, OWN // 8, product, (zero, zero))

    def total(v):
        return jnp.sum(jnp.sum(v, axis=0, keepdims=True), axis=1, keepdims=True)

    uu, uq = total(uu), total(uq)
    ratio = jnp.where(uu > 0, uq / uu, 0.0)

    def moment(i, carry):
        uw, ww, uy, wy = carry
        for t in range(DAYS):
            u, q, z = u_out[t, tile(i), :], q_out[t, tile(i), :], z_out[t, tile(i), :]
            w = q - ratio * u
            y = z - ratio * q
            uw, ww, uy, wy = uw + u * w, ww + w * w, uy + u * y, wy + w * y
        return uw, ww, uy, wy

    rest = [total(v) for v in lax.fori_loop(0, OWN // 8, moment, (zero,) * 4)]
    write_sets(sets, [uu] + rest + [ratio])


def write_sets(sets, values):
    row = lax.broadcasted_iota(jnp.int32, (8, 128), 0)
    out = jnp.zeros((8, 128), jnp.float32)
    for k, value in enumerate(values):
        out = jnp.where(row == k, value, out)
    for n in range(sets.shape[0]):
        sets[n] = out


def recentred(got):
    uu, uw, ww, uy, wy, ratio = (got[:, k, :] for k in range(6))

    def add(v):
        return jnp.sum(v, axis=0, keepdims=True)

    total = add(uu)
    centre = jnp.where(total > 0, add(uw + ratio * uu) / total, 0.0)
    e = ratio - centre
    uw_new = uw + e * uu
    ww_new = ww + e * (2.0 * uw + e * uu)
    uy_new = uy + e * uw + e * ratio * uu
    wy_new = wy + e * (ww + ratio * uw + uy) + e * e * (uw + ratio * uu)
    return total, add(uw_new), add(ww_new), add(uy_new), add(wy_new), centre


def regroup_kernel(got, sets):
    write_sets(sets, recentred(got))


def update_kernel(got, latent, u_in, q_in, z_in, updated, residual):
    m0, _, ww, _, wy, centre = (v[:, :1] for v in recentred(got))
    alpha0 = 1.0 / centre
    norm1 = alpha0 * alpha0 * ww
    beta = norm1 / m0
    curvature1 = alpha0 * alpha0 * wy - beta * beta * (centre * m0)
    alpha1 = norm1 / curvature1
    for i in range(OWN // 8):
        rows = slice(8 * i, 8 * i + 8)
        u, q, z = u_in[0, rows, :], q_in[0, rows, :], z_in[0, rows, :]
        residual1 = u - alpha0 * q
        direction1 = residual1 + beta * u
        image1 = (q - alpha0 * z) + beta * q
        updated[0, rows, :] = latent[0, rows, :] + (alpha0 * u + alpha1 * direction1)
        residual[0, rows, :] = residual1 - alpha1 * image1


def gathered(sets, axis):
    return lax.all_to_all(sets, axis, 0, 0)


def body(latent, counts, exposure, region_ids, coefficients):
    field = f32(DAYS, OWN, COLUMNS)
    spaces, times = lax.axis_size("space"), lax.axis_size("tm")
    at = jnp.stack(
        [lax.axis_index("space"), lax.axis_index("tm"), jnp.int32(spaces), jnp.int32(times)]
    ).astype(jnp.int32)

    intensity, excess, head, tail = pl.pallas_call(
        intensity_kernel,
        out_shape=(field, field, f32(EDGE, COLUMNS), f32(EDGE, COLUMNS)),
        in_specs=[SMEM, SMEM, VMEM, VMEM, VMEM],
        out_specs=(VMEM,) * 4,
        compiler_params=PARAMS,
        name="intensity",
    )(region_ids, coefficients, latent, counts, exposure)

    above = lax.ppermute(tail, "space", [(i, i + 1) for i in range(spaces - 1)])
    below = lax.ppermute(head, "space", [(i + 1, i) for i in range(spaces - 1)])

    frames = functools.partial(f32, FRAME, COLUMNS)
    res, inten, ends, inner, y_msg, c_msg = pl.pallas_call(
        residual_kernel,
        out_shape=(
            f32(DAYS, FRAME, COLUMNS),
            f32(DAYS, FRAME, COLUMNS),
            f32(2, FRAME, COLUMNS),
            f32(DAYS - 2, FRAME, COLUMNS),
            f32(MESSAGE, COLUMNS),
            f32(MESSAGE, COLUMNS),
        ),
        in_specs=[SMEM] + [VMEM] * 5,
        out_specs=(VMEM,) * 6,
        scratch_shapes=[pltpu.VMEM((DAYS, FRAME, COLUMNS), jnp.float32)] * 3,
        compiler_params=PARAMS,
        name="residual",
    )(at, latent, excess, intensity, above, below)

    across = [p for i in range(1, times - 1, 2) for p in ((i, i + 1), (i + 1, i))]
    within = [p for i in range(0, times - 1, 2) for p in ((i, i + 1), (i + 1, i))]
    y_got = lax.ppermute(y_msg, "tm", across)
    c_got = lax.ppermute(c_msg, "tm", within)

    six = pltpu.VMEM((DAYS + 2, FRAME, COLUMNS), jnp.float32)
    u, q, z, sets = pl.pallas_call(
        image_kernel,
        out_shape=(field, field, field, f32(times, 8, 128)),
        in_specs=[SMEM] + [VMEM] * 7,
        out_specs=(VMEM,) * 4,
        scratch_shapes=[six] * 4 + [pltpu.VMEM((8, FRAME, COLUMNS), jnp.float32)],
        compiler_params=PARAMS,
        name="image",
    )(at, res, inten, ends, inner, intensity, y_got, c_got)

    sets = pl.pallas_call(
        regroup_kernel,
        out_shape=f32(spaces, 8, 128),
        in_specs=[VMEM],
        out_specs=VMEM,
        name="regroup",
    )(gathered(sets, "tm"))

    day = pl.BlockSpec((1, OWN, COLUMNS), lambda t: (t, 0, 0))
    return pl.pallas_call(
        update_kernel,
        grid=(DAYS,),
        out_shape=(field, field),
        in_specs=[pl.BlockSpec((spaces, 8, 128), lambda t: (0, 0, 0))] + [day] * 4,
        out_specs=(day, day),
        compiler_params=PARAMS,
        name="update",
    )(gathered(sets, "space"), latent, u, q, z)


def solution(mesh):
    return jax.shard_map(
        body,
        mesh=mesh,
        in_specs=(
            P("tm", "space", None),
            P("tm", "space", None),
            P("tm", "space", None),
            P("space"),
            P(),
        ),
        out_specs=(P("tm", "space", None), P("tm", "space", None)),
        check_vma=False,
    )
```

time: 415 us -> 85.9 us (0.21)
  blocking collectives: 311 us -> 41.6 us
  starting transfers between devices: 53.4 us -> 13.5 us
  waiting for transfers between devices: 33.3 us -> 11.2 us
  Pallas kernels: 0 us -> 13.9 us
  other arithmetic: 9.68 us -> 0.08 us
  between operations: 5.07 us -> 0.71 us
    psum x3 -> x0, blocking collectives: 311 us -> none  [the longest x2 207 us: squares(): return lax.psum(jnp.sum(residual * residual), ('tm', 'space'))]
    all_to_all x0 -> x2, blocking collectives: none -> 41.6 us  [gathered(): return lax.all_to_all(sets, axis, 0, 0)]
    ppermute x18 -> x4, starting transfers between devices: 53.4 us -> 13.5 us  [the longest x1 5.89 us: body(): y_got = lax.ppermute(y_msg, 'tm', across)]
    ppermute x18 -> x4, waiting for transfers between devices: 33.3 us -> 11.2 us  [the longest x1 5.97 us: body(): y_got = lax.ppermute(y_msg, 'tm', across)]
    pallas_call x0 -> x5, Pallas kernels: none -> 13.9 us  [the longest x1 5.61 us: body(): pl.pallas_call(image_kernel, out_shape=(field, field, field, f32(times, 8...]
    unnamed x10 -> x12, local copies, waits for them, and re-layouts: 0.03 us -> 4.43 us
  transfers between devices with their start and end apart: 18 -> 4, of which waited for: 9 -> 3; matrix products, arithmetic and copies ran while one was open for 0% -> 0% of each run, Pallas kernels for 0% -> 0%
where the time goes in v2:
time: 85.9 us; the launch traced here: 85.4 us
  blocking collectives  41.6 us (48%)
  Pallas kernels  13.9 us (16%)
  starting transfers between devices  13.5 us (16%)
  waiting for transfers between devices  11.2 us (13%)
  local copies, waits for them, and re-layouts  4.43 us (5%)
    all_to_all x2, blocking collectives, gathered(): return lax.all_to_all(sets, axis, 0, 0)  41.6 us
    ppermute x1, waiting for transfers between devices, body(): y_got = lax.ppermute(y_msg, 'tm', across)  5.97 us
    ppermute x1, starting transfers between devices, body(): y_got = lax.ppermute(y_msg, 'tm', across)  5.89 us
    pallas_call x1, Pallas kernels, body(): pl.pallas_call(image_kernel, out_shape=(field, field, field, f32(times, 8...  5.61 us
    unnamed x12, local copies, waits for them, and re-layouts  4.43 us
    ppermute x1, starting transfers between devices, body(): above = lax.ppermute(tail, 'space', [(i, i + 1) for i in range(spaces - 1)])  4.38 us
    ppermute x1, waiting for transfers between devices, body(): below = lax.ppermute(head, 'space', [(i + 1, i) for i in range(spaces - 1)])  4 us
    pallas_call x1, Pallas kernels, body(): pl.pallas_call(residual_kernel, out_shape=(f32(DAYS, FRAME, COLUMNS), f32...  3.96 us
  transfers between devices with their start and end apart: 4, of which 3 were waited for; matrix products, arithmetic and copies ran while one was open for 0% of the time, Pallas kernels for 0%

profile of v2, /device:TPU:1, one launch (start us, length us, event | category | flops | bytes accessed | tf_op | source)
XLA Modules:
  0.0 85.4 jit_solution(6143743898915584869)
XLA Ops:
  0.6 0.0 copy-start
  0.6 1.0 %copy-done = f32[4,32,1024]{2,1,0:T(8,128)S(1)} copy-done((f32[4,32,1024]{2,1,0:T(8,128)S(1)}, f32[4,32,1024]{2,1,0:T(8,128)}, u32[]{:S(2)}) %copy-start) | copy-done | bytes 524312
  1.7 0.0 copy-start.2
  1.7 1.0 %copy-done.2 = s32[4,32,1024]{2,1,0:T(8,128)S(1)} copy-done((s32[4,32,1024]{2,1,0:T(8,128)S(1)}, s32[4,32,1024]{2,1,0:T(8,128)}, u32[]{:S(2)}) %copy-start.2) | copy-done | bytes 524312
  2.7 0.0 copy-start.3
  2.7 1.0 %copy-done.3 = f32[4,32,1024]{2,1,0:T(8,128)S(1)} copy-done((f32[4,32,1024]{2,1,0:T(8,128)S(1)}, f32[4,32,1024]{2,1,0:T(8,128)}, u32[]{:S(2)}) %copy-start.3) | copy-done | bytes 524312
  3.8 0.0 copy-start.4
  3.8 0.7 copy-done.4
  4.4 0.0 copy-start.5
  4.4 0.7 copy-done.5
  5.1 0.0 copy-start.1
  5.1 0.7 intensity.1
  5.8 4.4 %collective-permute-start = (f32[48,1024]{1,0:T(8,128)S(1)}, f32[48,1024]{1,0:T(8,128)S(1)}, u32[]{:S(2)}, u32[]{:S(2)}) collective-permute-start(f32[48,1024]{1,0:T(8,128)S(1)} %get-tuple-element.18), channel_id=1, source_target_pairs={{0,1},{1,2},{2,3},{3,4},{4,5},{5,6},{6,7},{7,8},{8,9},{9,10},{10,1... | collective-permute-start | bytes 589832 | tf_op jit(solution)/shard_map/ppermute | solution.py:310
  10.2 1.3 %collective-permute-start.1 = (f32[48,1024]{1,0:T(8,128)S(1)}, f32[48,1024]{1,0:T(8,128)S(1)}, u32[]{:S(2)}, u32[]{:S(2)}) collective-permute-start(f32[48,1024]{1,0:T(8,128)S(1)} %get-tuple-element.19), channel_id=1, source_target_pairs={{1,0},{2,1},{3,2},{4,3},{5,4},{6,5},{7,6},{8,7},{9,8},{10,9},{11,1... | collective-permute-start | bytes 589832 | tf_op jit(solution)/shard_map/ppermute | solution.py:311
  11.5 0.1 pad_add_fusion.at
  11.6 1.2 %collective-permute-done.above = f32[48,1024]{1,0:T(8,128)S(1)} collective-permute-done((f32[48,1024]{1,0:T(8,128)S(1)}, f32[48,1024]{1,0:T(8,128)S(1)}, u32[]{:S(2)}, u32[]{:S(2)}) %collective-permute-start) | collective-permute-done | bytes 196640 | tf_op jit(solution)/shard_map/ppermute | solution.py:310
  12.8 4.0 %collective-permute-done.1.below = f32[48,1024]{1,0:T(8,128)S(1)} collective-permute-done((f32[48,1024]{1,0:T(8,128)S(1)}, f32[48,1024]{1,0:T(8,128)S(1)}, u32[]{:S(2)}, u32[]{:S(2)}) %collective-permute-start.1) | collective-permute-done | bytes 196640 | tf_op jit(solution)/shard_map/ppermute | solution.py:311
  16.8 0.0 copy-done.1
  16.8 4.0 %residual.1 = (f32[4,48,1024]{2,1,0:T(8,128)S(1)}, f32[4,48,1024]{2,1,0:T(8,128)S(1)}, f32[2,48,1024]{2,1,0:T(8,128)S(1)}, f32[2,48,1024]{2,1,0:T(8,128)S(1)}, f...) custom-call(s32[4]{0:T(128)S(1)} %pad_add_fusion.at, f32[4,32,1024]{2,1,0:T(8,128)S(1)} %copy-done.1, ...), custom_call_target="tpu_custom_call" | custom-call | tf_op jit(solution)/shard_map/residual/pallas_call | solution.py:314
  20.8 5.9 %collective-permute-start.2 = (f32[152,1024]{1,0:T(8,128)S(1)}, f32[152,1024]{1,0:T(8,128)S(1)}, u32[]{:S(2)}, u32[]{:S(2)}) collective-permute-start(f32[152,1024]{1,0:T(8,128)S(1)} %get-tuple-element.24), channel_id=1, source_target_pairs={{16,32},{32,16},{48,64},{64,48},{80,96},{96,80},{112,128},{128,112... | collective-permute-start | bytes 1867784 | tf_op jit(solution)/shard_map/ppermute | solution.py:333
  26.7 1.9 %collective-permute-start.3 = (f32[152,1024]{1,0:T(8,128)S(1)}, f32[152,1024]{1,0:T(8,128)S(1)}, u32[]{:S(2)}, u32[]{:S(2)}) collective-permute-start(f32[152,1024]{1,0:T(8,128)S(1)} %get-tuple-element.25), channel_id=1, source_target_pairs={{0,16},{16,0},{32,48},{48,32},{64,80},{80,64},{96,112},{112,96},{1... | collective-permute-start | bytes 1867784 | tf_op jit(solution)/shard_map/ppermute | solution.py:334
  28.6 6.0 %collective-permute-done.2.y_msg = f32[152,1024]{1,0:T(8,128)S(1)} collective-permute-done((f32[152,1024]{1,0:T(8,128)S(1)}, f32[152,1024]{1,0:T(8,128)S(1)}, u32[]{:S(2)}, u32[]{:S(2)}) %collective-permute-start.2) | collective-permute-done | bytes 622624 | tf_op jit(solution)/shard_map/ppermute | solution.py:333
  34.6 0.0 collective-permute-done.3.c_msg
  34.6 5.6 %image.1 = (f32[4,32,1024]{2,1,0:T(8,128)S(1)}, f32[4,32,1024]{2,1,0:T(8,128)S(1)}, f32[4,32,1024]{2,1,0:T(8,128)S(1)}, f32[32,8,128]{2,1,0:T(8,128)S(1)}) custom-call(s32[4]{0:T(128)S(1)} %pad_add_fusion.at, f32[4,48,1024]{2,1,0:T(8,128)S(1)} %get-tuple-element.20.res, f32[4,48,1024]{2,1,0:T(8,128)S(1)} %get-tuple-element.21.inten, ...), custom_call_target="tpu_custom_call" | custom-call | tf_op jit(solution)/shard_map/image/pallas_call | solution.py:337
  40.2 15.6 %all_to_all.10.got = f32[32,8,128]{2,1,0:T(8,128)} all-to-all(f32[32,8,128]{2,1,0:T(8,128)S(1)} %get-tuple-element.26), channel_id=1, replica_groups=mesh['tm'=32,'space'=16] {'tm'}, dimensions={0} | all-to-all | bytes 262144 | tf_op jit(solution)/shard_map/all_to_all | solution.py:291
  55.8 1.7 %regroup.1 = f32[16,8,128]{2,1,0:T(8,128)} custom-call(f32[32,8,128]{2,1,0:T(8,128)} %all_to_all.10.got), custom_call_target="tpu_custom_call" | custom-call | tf_op jit(solution)/shard_map/regroup/pallas_call | solution.py:347
  57.5 26.0 %all_to_all.11.got = f32[16,8,128]{2,1,0:T(8,128)S(1)} all-to-all(f32[16,8,128]{2,1,0:T(8,128)} %regroup.1), channel_id=1, replica_groups=mesh['tm'=32,'space'=16] {'space'}, dimensions={0} | all-to-all | bytes 131072 | tf_op jit(solution)/shard_map/all_to_all | solution.py:291
  83.5 2.0 %update.1 = (f32[4,32,1024]{2,1,0:T(8,128)}, f32[4,32,1024]{2,1,0:T(8,128)}) custom-call(f32[16,8,128]{2,1,0:T(8,128)S(1)} %all_to_all.11.got, f32[4,32,1024]{2,1,0:T(8,128)S(1)} %copy-done.1, f32[4,32,1024]{2,1,0:T(8,128)S(1)} %get-tuple-element.27.u_in, f32[4,32,1024]{2,1,0:T(8,128)S(1)} %get-tuple-element.28.q_in, f32[4,32,1024]{2,1,0:T(8,128)S(1)} %get-tuple-element.29.z_in), custom_call_target="tpu_custom_call" | custom-call | tf_op jit(solution)/shard_map/update/pallas_call | solution.py:356
Async XLA Ops:
  0.6 1.0 %copy-start = (f32[4,32,1024]{2,1,0:T(8,128)S(1)}, f32[4,32,1024]{2,1,0:T(8,128)}, u32[]{:S(2)}) copy-start(f32[4,32,1024]{2,1,0:T(8,128)} %latent.5) | copy-start | bytes 1572868
  1.7 1.0 %copy-start.2 = (s32[4,32,1024]{2,1,0:T(8,128)S(1)}, s32[4,32,1024]{2,1,0:T(8,128)}, u32[]{:S(2)}) copy-start(s32[4,32,1024]{2,1,0:T(8,128)} %counts.1) | copy-start | bytes 1572868
  2.7 1.0 %copy-start.3 = (f32[4,32,1024]{2,1,0:T(8,128)S(1)}, f32[4,32,1024]{2,1,0:T(8,128)}, u32[]{:S(2)}) copy-start(f32[4,32,1024]{2,1,0:T(8,128)} %exposure.1) | copy-start | bytes 1572868
  3.8 0.7 copy-start.4
  4.4 0.7 copy-start.5
  5.1 11.7 %copy-start.1 = (f32[4,32,1024]{2,1,0:T(8,128)S(1)}, f32[4,32,1024]{2,1,0:T(8,128)}, u32[]{:S(2)}) copy-start(f32[4,32,1024]{2,1,0:T(8,128)} %latent.5) | copy-start | bytes 1572868
  5.8 7.0 %collective-permute-start = (f32[48,1024]{1,0:T(8,128)S(1)}, f32[48,1024]{1,0:T(8,128)S(1)}, u32[]{:S(2)}, u32[]{:S(2)}) collective-permute-start(f32[48,1024]{1,0:T(8,128)S(1)} %get-tuple-element.18), channel_id=1, source_target_pairs={{0,1},{1,2},{2,3},{3,4},{4,5},{5,6},{6,7},{7,8},{8,9},{9,10},{10,1... | collective-permute-start | bytes 589832 | tf_op jit(solution)/shard_map/ppermute | solution.py:310
  10.2 6.6 %collective-permute-start.1 = (f32[48,1024]{1,0:T(8,128)S(1)}, f32[48,1024]{1,0:T(8,128)S(1)}, u32[]{:S(2)}, u32[]{:S(2)}) collective-permute-start(f32[48,1024]{1,0:T(8,128)S(1)} %get-tuple-element.19), channel_id=1, source_target_pairs={{1,0},{2,1},{3,2},{4,3},{5,4},{6,5},{7,6},{8,7},{9,8},{10,9},{11,1... | collective-permute-start | bytes 589832 | tf_op jit(solution)/shard_map/ppermute | solution.py:311
  20.8 13.8 %collective-permute-start.2 = (f32[152,1024]{1,0:T(8,128)S(1)}, f32[152,1024]{1,0:T(8,128)S(1)}, u32[]{:S(2)}, u32[]{:S(2)}) collective-permute-start(f32[152,1024]{1,0:T(8,128)S(1)} %get-tuple-element.24), channel_id=1, source_target_pairs={{16,32},{32,16},{48,64},{64,48},{80,96},{96,80},{112,128},{128,112... | collective-permute-start | bytes 1867784 | tf_op jit(solution)/shard_map/ppermute | solution.py:333
  26.7 7.9 %collective-permute-start.3 = (f32[152,1024]{1,0:T(8,128)S(1)}, f32[152,1024]{1,0:T(8,128)S(1)}, u32[]{:S(2)}, u32[]{:S(2)}) collective-permute-start(f32[152,1024]{1,0:T(8,128)S(1)} %get-tuple-element.25), channel_id=1, source_target_pairs={{0,16},{16,0},{32,48},{48,32},{64,80},{80,64},{96,112},{112,96},{1... | collective-permute-start | bytes 1867784 | tf_op jit(solution)/shard_map/ppermute | solution.py:334

commit v3 on v0

v3 whole, which is shorter than its diff:
```python
import functools

import jax
import jax.numpy as jnp
from jax import lax
from jax.experimental import pallas as pl
from jax.experimental.pallas import tpu as pltpu
from jax.sharding import PartitionSpec as P

kappa_square = 0.3
time_corr = 0.9
prior_scale = 0.05

COUPLE = prior_scale * time_corr
INNER = prior_scale * (1.0 + time_corr * time_corr)
DIAG = kappa_square + 4.0

DAYS, OWN, COLUMNS = 4, 32, 1024
TILES = OWN // 8 + 2
FRAME = 8 * TILES
BOTTOM = TILES - 1
OWN_TILES = range(1, BOTTOM)
REGION_ROWS = 4
EDGE = 8 * (DAYS + DAYS // 2)
MESSAGE_TILES = 2 * (OWN // 8 + 1) + 2 * (OWN // 8) + 1
S_AT, R_AT, Q_AT, I_AT, H_AT = 0, 5, 10, 14, 18

VMEM = pl.BlockSpec(memory_space=pltpu.VMEM)
HBM = pl.BlockSpec(memory_space=pltpu.HBM)
PARAMS = pltpu.CompilerParams(vmem_limit_bytes=40 * 1024 * 1024)


def f32(*shape):
    return jax.ShapeDtypeStruct(shape, jnp.float32)


def rows(i):
    return slice(8 * i, 8 * i + 8)


def row_iota():
    return lax.broadcasted_iota(jnp.int32, (8, COLUMNS), 0)


def up_roll(v, k):
    return pltpu.roll(v, k, 0)


def places():
    sp, tm = lax.axis_index("space"), lax.axis_index("tm")
    spaces, times = lax.axis_size("space"), lax.axis_size("tm")
    return sp > 0, sp < spaces - 1, tm > 0, tm < times - 1, lax.rem(tm, 2) == 0


def framed(ref):
    return lambda s, i: ref[s, rows(i), :]


def apply_k(load, dst, planes, has_above, has_below, tiles=range(TILES)):
    row = row_iota()
    lane = lax.broadcasted_iota(jnp.int32, (8, 128), 1)
    for s, d in planes:
        cur = load(s, tiles[0])
        prev = load(s, tiles[0] - 1) if tiles[0] > 0 else cur
        for i in tiles:
            nxt = load(s, i + 1) if i < BOTTOM else cur
            up = up_roll(jnp.where(row == 7, prev, cur), 1)
            down = up_roll(jnp.where(row == 0, nxt, cur), 7)
            left = pltpu.roll(cur, 1, 1)
            right = pltpu.roll(cur, COLUMNS - 1, 1)
            left = jnp.concatenate([jnp.where(lane == 0, 0.0, left[:, :128]), left[:, 128:]], axis=1)
            right = jnp.concatenate(
                [right[:, :-128], jnp.where(lane == 127, 0.0, right[:, -128:])], axis=1
            )
            out = DIAG * cur - ((up + down) + (left + right))
            if i == 0:
                out = jnp.where(has_above, out, 0.0)
            if i == BOTTOM:
                out = jnp.where(has_below, out, 0.0)
            dst[d, rows(i), :] = out
            prev, cur = cur, nxt


def day_weights(has_before, has_after):
    first = jnp.where(has_before, INNER, prior_scale).astype(jnp.float32)
    last = jnp.where(has_after, INNER, prior_scale).astype(jnp.float32)
    return [first] + [jnp.float32(INNER)] * (DAYS - 2) + [last]


def intensity_kernel(
    ids_in, coef_in, latent, counts, exposure, lat, exc, inten, head, tail, ids, coef, cnt, exposed, sems
):
    small = [
        pltpu.make_async_copy(ids_in, ids, sems.at[3 * DAYS]),
        pltpu.make_async_copy(coef_in, coef, sems.at[3 * DAYS + 1]),
    ]
    days = [
        (
            pltpu.make_async_copy(latent.at[t], lat.at[t], sems.at[3 * t]),
            pltpu.make_async_copy(exposure.at[t], exposed.at[t], sems.at[3 * t + 1]),
            pltpu.make_async_copy(counts.at[t], cnt.at[t], sems.at[3 * t + 2]),
        )
        for t in range(DAYS)
    ]
    for copy in small:
        copy.start()
    for copies in days:
        for copy in copies:
            copy.start()
    for copy in small:
        copy.wait()
    row = row_iota()
    blocks = 8 // REGION_ROWS
    offsets = [
        jnp.where(row < REGION_ROWS, coef[ids[blocks * i]], coef[ids[blocks * i + 1]])
        for i in range(OWN // 8)
    ]
    for t in range(DAYS):
        for copy in days[t]:
            copy.wait()
        for i in range(OWN // 8):
            value = exposed[t, rows(i), :] * jnp.exp(offsets[i] + lat[t, rows(i), :])
            inten[t, rows(i), :] = value
            exc[t, rows(i), :] = value - cnt[t, rows(i), :].astype(jnp.float32)
    last = OWN // 8 - 1
    for t in range(DAYS):
        tail[rows(t), :] = jnp.where(row < 2, up_roll(inten[t, rows(last), :], 2), lat[t, rows(last), :])
        head[rows(t), :] = jnp.where(row >= 6, up_roll(inten[t, rows(0), :], 6), lat[t, rows(0), :])
    for k in range(DAYS // 2):
        a, b = 2 * k, 2 * k + 1
        tail[rows(DAYS + k), :] = jnp.where(
            row >= 4, exc[a, rows(last), :], up_roll(exc[b, rows(last), :], 4)
        )
        head[rows(DAYS + k), :] = jnp.where(row < 4, exc[a, rows(0), :], up_roll(exc[b, rows(0), :], 4))


def residual_kernel(latent, inten, exc, above, below, lat, res, inner, y_msg, c_msg, tmp):
    has_above, has_below, has_before, has_after, even = places()
    row = row_iota()

    def field(t, i):
        if i in OWN_TILES:
            return latent[t, rows(i - 1), :]
        return (above if i == 0 else below)[rows(t), :]

    same = [(t, t) for t in range(DAYS)]
    apply_k(field, tmp, same, has_above, has_below)
    apply_k(framed(tmp), lat, same, has_above, has_below)
    weight = day_weights(has_before, has_after)

    for i in range(TILES):
        s = [lat[t, rows(i), :] for t in range(DAYS)]
        for t in range(DAYS):
            if i in (0, BOTTOM):
                excess = (above if i == 0 else below)[rows(DAYS + t // 2), :]
                excess = up_roll(excess, 4) if t % 2 else excess
            else:
                excess = exc[t, rows(i - 1), :]
            value = weight[t] * s[t] + excess
            if t > 0:
                value = value - COUPLE * s[t - 1]
            if t < DAYS - 1:
                value = value - COUPLE * s[t + 1]
            res[t, rows(i), :] = -value
    middle = range(DAYS - 2)
    apply_k(framed(res), tmp, [(k + 1, k) for k in middle], has_above, has_below)
    apply_k(framed(tmp), inner, [(k, k) for k in middle], has_above, has_below)

    def send(at, before, after):
        y_msg[rows(at), :] = jnp.where(even, before, after)
        c_msg[rows(at), :] = jnp.where(even, after, before)

    def halo(field, day):
        return jnp.where(row < 4, field[day, rows(BOTTOM), :], field[day, rows(0), :])

    first, last = 0, DAYS - 1
    for i in OWN_TILES:
        send(S_AT + i, lat[first, rows(i), :], lat[last, rows(i), :])
        send(R_AT + i, res[first, rows(i), :], res[last, rows(i), :])
        send(Q_AT + i - 1, -COUPLE * inner[0, rows(i), :], -COUPLE * inner[DAYS - 3, rows(i), :])
        send(I_AT + i - 1, inten[first, rows(i - 1), :], inten[last, rows(i - 1), :])
    send(S_AT, halo(lat, first), halo(lat, last))
    send(R_AT, halo(res, first), halo(res, last))
    outer = (row < 2) | (row >= 6)

    def slim(day, near):
        wanted = jnp.where(row < 4, up_roll(above[rows(day), :], 2), up_roll(below[rows(day), :], 6))
        return jnp.where(outer, -COUPLE * halo(inner, near), wanted)

    send(H_AT, slim(first, 0), slim(last, DAYS - 3))


def image_kernel(
    res, inner, lat, inten, above, below, y_msg, c_msg, u_out, q_out, z_out, sets, r6, q6, f6, tmp
):
    has_above, has_below, has_before, has_after, even = places()
    weight = day_weights(has_before, has_after)
    last = DAYS + 1

    def got(at):
        y, c = y_msg[rows(at), :], c_msg[rows(at), :]
        return jnp.where(even, y, c), jnp.where(even, c, y)

    for i in range(TILES):
        k = i if i in OWN_TILES else 0
        s_before, s_after = got(S_AT + k)
        r_before, r_after = got(R_AT + k)
        r6[0, rows(i), :] = jnp.where(has_before, r_before + COUPLE * lat[0, rows(i), :], 0.0)
        r6[last, rows(i), :] = jnp.where(has_after, r_after + COUPLE * lat[DAYS - 1, rows(i), :], 0.0)
        r6[1, rows(i), :] = res[0, rows(i), :] + COUPLE * s_before
        r6[DAYS, rows(i), :] = res[DAYS - 1, rows(i), :] + COUPLE * s_after
    outer = [(0, 0), (1, 1), (DAYS, DAYS), (last, last)]
    apply_k(framed(r6), tmp, outer, has_above, has_below)
    apply_k(framed(tmp), f6, outer, has_above, has_below)

    def residual(t, i):
        return r6[t, rows(i), :] if (t, t) in outer else res[t - 1, rows(i), :]

    def intensity(t, i):
        if i in OWN_TILES:
            return inten[t, rows(i - 1), :]
        return up_roll(above[rows(t), :], 6) if i == 0 else up_roll(below[rows(t), :], 2)

    for i in range(TILES):
        f = [
            f6[t, rows(i), :] if (t, t) in outer else inner[t - 2, rows(i), :]
            for t in range(DAYS + 2)
        ]
        r = [residual(t, i) for t in range(DAYS + 2)]
        for t in range(DAYS):
            q6[t + 1, rows(i), :] = (
                weight[t] * f[t + 1] - COUPLE * (f[t] + f[t + 2]) + intensity(t, i) * r[t + 1]
            )
        if i in OWN_TILES:
            q_side, i_side = got(Q_AT + i - 1), got(I_AT + i - 1)
        else:
            q_side = got(H_AT)
            i_side = [up_roll(v, 4) for v in q_side]
        before = INNER * f[0] - COUPLE * f[1] + q_side[0] + i_side[0] * r[0]
        after = INNER * f[last] - COUPLE * f[DAYS] + q_side[1] + i_side[1] * r[last]
        q6[0, rows(i), :] = jnp.where(has_before, before, 0.0)
        q6[last, rows(i), :] = jnp.where(has_after, after, 0.0)
    every = [(t, t) for t in range(DAYS + 2)]
    apply_k(framed(q6), tmp, every, has_above, has_below)
    apply_k(framed(tmp), f6, every, has_above, has_below, OWN_TILES)
    zero = jnp.zeros((8, COLUMNS), jnp.float32)

    uu = uq = zero
    for i in OWN_TILES:
        f = [f6[t, rows(i), :] for t in range(DAYS + 2)]
        for t in range(DAYS):
            q, u = q6[t + 1, rows(i), :], residual(t + 1, i)
            z = weight[t] * f[t + 1] - COUPLE * (f[t] + f[t + 2]) + intensity(t, i) * q
            z_out[t, rows(i - 1), :] = z
            q_out[t, rows(i - 1), :] = q
            u_out[t, rows(i - 1), :] = u
            uu = uu + u * u
            uq = uq + u * q

    def total(v):
        return jnp.sum(jnp.sum(v, axis=0, keepdims=True), axis=1, keepdims=True)

    uu, uq = total(uu), total(uq)
    ratio = jnp.where(uu > 0, uq / uu, 0.0)
    uw = ww = uy = wy = zero
    for i in range(OWN // 8):
        for t in range(DAYS):
            u, q, z = u_out[t, rows(i), :], q_out[t, rows(i), :], z_out[t, rows(i), :]
            w = q - ratio * u
            y = z - ratio * q
            uw, ww, uy, wy = uw + u * w, ww + w * w, uy + u * y, wy + w * y
    write_sets(sets, [uu, total(uw), total(ww), total(uy), total(wy), ratio])


def write_sets(sets, values):
    row = lax.broadcasted_iota(jnp.int32, (8, 128), 0)
    out = jnp.zeros((8, 128), jnp.float32)
    for k, value in enumerate(values):
        out = jnp.where(row == k, value, out)
    for n in range(sets.shape[0] // 8):
        sets[rows(n), :] = out


def recentred(got):
    senders = got.shape[0] // 8
    uu, uw, ww, uy, wy, ratio = (got[pl.ds(k, senders, 8), :] for k in range(6))

    def add(v):
        return jnp.sum(v, axis=0, keepdims=True)

    total = add(uu)
    centre = jnp.where(total > 0, add(uw + ratio * uu) / total, 0.0)
    e = ratio - centre
    uw_new = uw + e * uu
    ww_new = ww + e * (2.0 * uw + e * uu)
    uy_new = uy + e * uw + e * ratio * uu
    wy_new = wy + e * (ww + ratio * uw + uy) + e * e * (uw + ratio * uu)
    return total, add(uw_new), add(ww_new), add(uy_new), add(wy_new), centre


def regroup_kernel(got, sets):
    write_sets(sets, recentred(got))


def update_kernel(got, latent, u_in, q_in, z_in, updated, residual, factors):
    @pl.when(pl.program_id(0) == 0)
    def _():
        m0, _, ww, _, wy, centre = recentred(got)
        alpha0 = 1.0 / centre
        norm1 = alpha0 * alpha0 * ww
        beta = norm1 / m0
        curvature1 = alpha0 * alpha0 * wy - beta * beta * (centre * m0)
        factors[0:1, :] = alpha0
        factors[1:2, :] = beta
        factors[2:3, :] = norm1 / curvature1

    alpha0, beta, alpha1 = (factors[k : k + 1, 0:1] for k in range(3))
    for i in range(OWN // 8):
        u, q, z = u_in[0, rows(i), :], q_in[0, rows(i), :], z_in[0, rows(i), :]
        residual1 = u - alpha0 * q
        direction1 = residual1 + beta * u
        image1 = (q - alpha0 * z) + beta * q
        updated[0, rows(i), :] = latent[0, rows(i), :] + (alpha0 * u + alpha1 * direction1)
        residual[0, rows(i), :] = residual1 - alpha1 * image1


def gathered(sets, axis):
    count = lax.axis_size(axis)
    got = lax.all_to_all(sets.reshape(count, 8, 128), axis, 0, 0)
    return got.reshape(8 * count, 128)


def body(latent, counts, exposure, region_ids, coefficients):
    spaces, times = lax.axis_size("space"), lax.axis_size("tm")
    field, four = f32(DAYS, OWN, COLUMNS), f32(DAYS, FRAME, COLUMNS)
    edge, message = f32(EDGE, COLUMNS), f32(8 * MESSAGE_TILES, COLUMNS)

    def vmem(shape, dtype=jnp.float32):
        return pltpu.VMEM(shape, dtype)

    lat, exc, inten, head, tail = pl.pallas_call(
        intensity_kernel,
        out_shape=(field, field, field, edge, edge),
        in_specs=[HBM] * 5,
        out_specs=(VMEM,) * 5,
        scratch_shapes=[
            pltpu.SMEM(region_ids.shape, jnp.int32),
            pltpu.SMEM(coefficients.shape, jnp.float32),
            vmem(counts.shape, jnp.int32),
            vmem(exposure.shape),
            pltpu.SemaphoreType.DMA((3 * DAYS + 2,)),
        ],
        compiler_params=PARAMS,
        name="intensity",
    )(region_ids, coefficients, latent, counts, exposure)

    above = lax.ppermute(tail, "space", [(i, i + 1) for i in range(spaces - 1)])
    below = lax.ppermute(head, "space", [(i + 1, i) for i in range(spaces - 1)])

    spatial, res, inner, y_msg, c_msg = pl.pallas_call(
        residual_kernel,
        out_shape=(four, four, f32(DAYS - 2, FRAME, COLUMNS), message, message),
        in_specs=[VMEM] * 5,
        out_specs=(VMEM,) * 5,
        scratch_shapes=[vmem(four.shape)],
        compiler_params=PARAMS,
        name="residual",
    )(lat, inten, exc, above, below)

    across = [p for i in range(1, times - 1, 2) for p in ((i, i + 1), (i + 1, i))]
    within = [p for i in range(0, times - 1, 2) for p in ((i, i + 1), (i + 1, i))]
    y_got = lax.ppermute(y_msg, "tm", across)
    c_got = lax.ppermute(c_msg, "tm", within)

    six = vmem((DAYS + 2, FRAME, COLUMNS))
    u, q, z, sets = pl.pallas_call(
        image_kernel,
        out_shape=(field, field, field, f32(8 * times, 128)),
        in_specs=[VMEM] * 8,
        out_specs=(VMEM,) * 4,
        scratch_shapes=[six] * 4,
        compiler_params=PARAMS,
        name="image",
    )(res, inner, spatial, inten, above, below, y_got, c_got)

    sets = pl.pallas_call(
        regroup_kernel,
        out_shape=f32(8 * spaces, 128),
        in_specs=[VMEM],
        out_specs=VMEM,
        name="regroup",
    )(gathered(sets, "tm"))

    day = pl.BlockSpec((1, OWN, COLUMNS), lambda t: (t, 0, 0))
    return pl.pallas_call(
        update_kernel,
        grid=(DAYS,),
        out_shape=(field, field),
        in_specs=[pl.BlockSpec((8 * spaces, 128), lambda t: (0, 0)), day, day, day, day],
        out_specs=(day, day),
        scratch_shapes=[vmem((8, 128))],
        compiler_params=PARAMS,
        name="update",
    )(gathered(sets, "space"), latent, u, q, z)


def solution(mesh):
    return jax.shard_map(
        body,
        mesh=mesh,
        in_specs=(
            P("tm", "space", None),
            P("tm", "space", None),
            P("tm", "space", None),
            P("space"),
            P(),
        ),
        out_specs=(P("tm", "space", None), P("tm", "space", None)),
        check_vma=False,
    )
```

time: 415 us -> 81.8 us (0.20)
  blocking collectives: 311 us -> 41.7 us
  starting transfers between devices: 53.4 us -> 13.5 us
  waiting for transfers between devices: 33.3 us -> 11.3 us
  Pallas kernels: 0 us -> 9.69 us
  other arithmetic: 9.68 us -> 0 us
  between operations: 5.07 us -> 0.71 us
    psum x3 -> x0, blocking collectives: 311 us -> none  [the longest x2 207 us: squares(): return lax.psum(jnp.sum(residual * residual), ('tm', 'space'))]
    all_to_all x0 -> x2, blocking collectives: none -> 41.7 us  [gathered(): got = lax.all_to_all(sets.reshape(count, 8, 128), axis, 0, 0)]
    ppermute x18 -> x4, starting transfers between devices: 53.4 us -> 13.5 us  [the longest x1 5.89 us: body(): y_got = lax.ppermute(y_msg, 'tm', across)]
    ppermute x18 -> x4, waiting for transfers between devices: 33.3 us -> 11.3 us  [the longest x1 5.97 us: body(): y_got = lax.ppermute(y_msg, 'tm', across)]
    pallas_call x0 -> x5, Pallas kernels: none -> 9.69 us  [the longest x1 2.62 us: body(): pl.pallas_call(image_kernel, out_shape=(field, field, field, f32(8 * time...]
    unnamed x10 -> x12, local copies, waits for them, and re-layouts: 0.03 us -> 4.43 us
  transfers between devices with their start and end apart: 18 -> 4, of which waited for: 9 -> 3; matrix products, arithmetic and copies ran while one was open for 0% -> 0% of each run, Pallas kernels for 0% -> 0%
where the time goes in v3:
time: 81.8 us; the launch traced here: 81.3 us
  blocking collectives  41.7 us (51%)
  starting transfers between devices  13.5 us (17%)
  waiting for transfers between devices  11.3 us (14%)
  Pallas kernels  9.69 us (12%)
  local copies, waits for them, and re-layouts  4.43 us (5%)
    all_to_all x2, blocking collectives, gathered(): got = lax.all_to_all(sets.reshape(count, 8, 128), axis, 0, 0)  41.7 us
    ppermute x1, waiting for transfers between devices, body(): y_got = lax.ppermute(y_msg, 'tm', across)  5.97 us
    ppermute x1, starting transfers between devices, body(): y_got = lax.ppermute(y_msg, 'tm', across)  5.89 us
    unnamed x12, local copies, waits for them, and re-layouts  4.43 us
    ppermute x1, starting transfers between devices, body(): above = lax.ppermute(tail, 'space', [(i, i + 1) for i in range(spaces - 1)])  4.38 us
    ppermute x1, waiting for transfers between devices, body(): below = lax.ppermute(head, 'space', [(i + 1, i) for i in range(spaces - 1)])  4 us
    pallas_call x1, Pallas kernels, body(): pl.pallas_call(image_kernel, out_shape=(field, field, field, f32(8 * time...  2.62 us
    pallas_call x1, Pallas kernels, body(): pl.pallas_call(intensity_kernel, out_shape=(field, field, field, edge, ed...  2.34 us
  transfers between devices with their start and end apart: 4, of which 3 were waited for; matrix products, arithmetic and copies ran while one was open for 0% of the time, Pallas kernels for 0%

profile of v3, /device:TPU:1, one launch (start us, length us, event | category | flops | bytes accessed | tf_op | source)
XLA Modules:
  0.0 81.3 jit_solution(5939387608996652177)
XLA Ops:
  0.6 0.0 copy-start
  0.6 1.0 %copy-done = f32[4,32,1024]{2,1,0:T(8,128)S(1)} copy-done((f32[4,32,1024]{2,1,0:T(8,128)S(1)}, f32[4,32,1024]{2,1,0:T(8,128)}, u32[]{:S(2)}) %copy-start) | copy-done | bytes 524312
  1.7 0.0 copy-start.2
  1.7 1.0 %copy-done.2 = s32[4,32,1024]{2,1,0:T(8,128)S(1)} copy-done((s32[4,32,1024]{2,1,0:T(8,128)S(1)}, s32[4,32,1024]{2,1,0:T(8,128)}, u32[]{:S(2)}) %copy-start.2) | copy-done | bytes 524312
  2.7 0.0 copy-start.3
  2.7 1.0 %copy-done.3 = f32[4,32,1024]{2,1,0:T(8,128)S(1)} copy-done((f32[4,32,1024]{2,1,0:T(8,128)S(1)}, f32[4,32,1024]{2,1,0:T(8,128)}, u32[]{:S(2)}) %copy-start.3) | copy-done | bytes 524312
  3.8 0.0 copy-start.4
  3.8 0.7 copy-done.4
  4.4 0.0 copy-start.5
  4.4 0.7 copy-done.5
  5.1 2.3 %intensity.1 = (f32[4,32,1024]{2,1,0:T(8,128)S(1)}, f32[4,32,1024]{2,1,0:T(8,128)S(1)}, f32[4,32,1024]{2,1,0:T(8,128)S(1)}, f32[48,1024]{1,0:T(8,128)S(1)}, f32[48,1024]{1,0:T(8,128)S(1)}) custom-call(s32[8]{0:T(128)S(1)} %copy-done.4, f32[16]{0:T(128)S(1)} %copy-done.5, f32[4,32,1024]{2,1,0:T(8,128)S(1)} %copy-done, s32[4,32,1024]{2,1,0:T(8,128)S(1)} %copy-done.2, ...), custom_call_target="tpu_custom_call" | custom-call | tf_op jit(solution)/shard_map/intensity/pallas_call | solution.py:341
  7.4 4.4 %collective-permute-start = (f32[48,1024]{1,0:T(8,128)S(1)}, f32[48,1024]{1,0:T(8,128)S(1)}, u32[]{:S(2)}, u32[]{:S(2)}) collective-permute-start(f32[48,1024]{1,0:T(8,128)S(1)} %get-tuple-element.19), channel_id=1, source_target_pairs={{0,1},{1,2},{2,3},{3,4},{4,5},{5,6},{6,7},{7,8},{8,9},{9,10},{10,1... | collective-permute-start | bytes 589832 | tf_op jit(solution)/shard_map/ppermute | solution.py:357
  11.8 1.3 %collective-permute-start.1 = (f32[48,1024]{1,0:T(8,128)S(1)}, f32[48,1024]{1,0:T(8,128)S(1)}, u32[]{:S(2)}, u32[]{:S(2)}) collective-permute-start(f32[48,1024]{1,0:T(8,128)S(1)} %get-tuple-element.20), channel_id=1, source_target_pairs={{1,0},{2,1},{3,2},{4,3},{5,4},{6,5},{7,6},{8,7},{9,8},{10,9},{11,1... | collective-permute-start | bytes 589832 | tf_op jit(solution)/shard_map/ppermute | solution.py:358
  13.1 1.3 %collective-permute-done.above = f32[48,1024]{1,0:T(8,128)S(1)} collective-permute-done((f32[48,1024]{1,0:T(8,128)S(1)}, f32[48,1024]{1,0:T(8,128)S(1)}, u32[]{:S(2)}, u32[]{:S(2)}) %collective-permute-start) | collective-permute-done | bytes 196640 | tf_op jit(solution)/shard_map/ppermute | solution.py:357
  14.4 4.0 %collective-permute-done.1.below = f32[48,1024]{1,0:T(8,128)S(1)} collective-permute-done((f32[48,1024]{1,0:T(8,128)S(1)}, f32[48,1024]{1,0:T(8,128)S(1)}, u32[]{:S(2)}, u32[]{:S(2)}) %collective-permute-start.1) | collective-permute-done | bytes 196640 | tf_op jit(solution)/shard_map/ppermute | solution.py:358
  18.4 1.4 %residual.1 = (f32[4,48,1024]{2,1,0:T(8,128)S(1)}, f32[4,48,1024]{2,1,0:T(8,128)S(1)}, f32[2,48,1024]{2,1,0:T(8,128)S(1)}, f32[152,1024]{1,0:T(8,128)S(1)}, f32[152,1024]{1,0:T(8,128)S(1)}) custom-call(f32[4,32,1024]{2,1,0:T(8,128)S(1)} %get-tuple-element.16.latent, f32[4,32,1024]{2,1,0:T(8,128)S(1)} %get-tuple-element.17.inten, ...), custom_call_target="tpu_custom_call" | custom-call | tf_op jit(solution)/shard_map/residual/pallas_call | solution.py:360
  19.8 5.9 %collective-permute-start.2 = (f32[152,1024]{1,0:T(8,128)S(1)}, f32[152,1024]{1,0:T(8,128)S(1)}, u32[]{:S(2)}, u32[]{:S(2)}) collective-permute-start(f32[152,1024]{1,0:T(8,128)S(1)} %get-tuple-element.24), channel_id=1, source_target_pairs={{16,32},{32,16},{48,64},{64,48},{80,96},{96,80},{112,128},{128,112... | collective-permute-start | bytes 1867784 | tf_op jit(solution)/shard_map/ppermute | solution.py:372
  25.7 1.9 %collective-permute-start.3 = (f32[152,1024]{1,0:T(8,128)S(1)}, f32[152,1024]{1,0:T(8,128)S(1)}, u32[]{:S(2)}, u32[]{:S(2)}) collective-permute-start(f32[152,1024]{1,0:T(8,128)S(1)} %get-tuple-element.25), channel_id=1, source_target_pairs={{0,16},{16,0},{32,48},{48,32},{64,80},{80,64},{96,112},{112,96},{1... | collective-permute-start | bytes 1867784 | tf_op jit(solution)/shard_map/ppermute | solution.py:373
  27.6 6.0 %collective-permute-done.2.y_msg = f32[152,1024]{1,0:T(8,128)S(1)} collective-permute-done((f32[152,1024]{1,0:T(8,128)S(1)}, f32[152,1024]{1,0:T(8,128)S(1)}, u32[]{:S(2)}, u32[]{:S(2)}) %collective-permute-start.2) | collective-permute-done | bytes 622624 | tf_op jit(solution)/shard_map/ppermute | solution.py:372
  33.6 0.0 collective-permute-done.3.c_msg
  33.6 2.6 %image.1 = (f32[4,32,1024]{2,1,0:T(8,128)S(1)}, f32[4,32,1024]{2,1,0:T(8,128)S(1)}, f32[4,32,1024]{2,1,0:T(8,128)S(1)}, f32[256,128]{1,0:T(8,128)S(1)}) custom-call(f32[4,48,1024]{2,1,0:T(8,128)S(1)} %get-tuple-element.21.res, f32[2,48,1024]{2,1,0:T(8,128)S(1)} %get-tuple-element.22.inner, f32[4,48,1024]{2,1,0:T(8,128)S(1)} %get-tuple-element.23.lat, ...), custom_call_target="tpu_custom_call" | custom-call | tf_op jit(solution)/shard_map/image/pallas_call | solution.py:376
  36.2 0.0 copy-start.1
  36.2 15.8 %all_to_all.10 = f32[32,8,128]{2,1,0:T(8,128)} all-to-all(f32[32,8,128]{2,1,0:T(8,128)S(1)} %bitcast.5), channel_id=1, replica_groups=mesh['tm'=32,'space'=16] {'tm'}, dimensions={0} | all-to-all | bytes 262144 | tf_op jit(solution)/shard_map/all_to_all | solution.py:329
  52.0 1.6 %regroup.1 = f32[128,128]{1,0:T(8,128)} custom-call(f32[256,128]{1,0:T(8,128)} %bitcast.6), custom_call_target="tpu_custom_call" | custom-call | tf_op jit(solution)/shard_map/regroup/pallas_call | solution.py:386
  53.6 26.0 %all_to_all.11 = f32[16,8,128]{2,1,0:T(8,128)S(1)} all-to-all(f32[16,8,128]{2,1,0:T(8,128)} %bitcast.7), channel_id=1, replica_groups=mesh['tm'=32,'space'=16] {'space'}, dimensions={0} | all-to-all | bytes 131072 | tf_op jit(solution)/shard_map/all_to_all | solution.py:329
  79.6 0.0 copy-done.1
  79.6 1.8 %update.1 = (f32[4,32,1024]{2,1,0:T(8,128)}, f32[4,32,1024]{2,1,0:T(8,128)}) custom-call(f32[128,128]{1,0:T(8,128)S(1)} %bitcast.4, f32[4,32,1024]{2,1,0:T(8,128)S(1)} %copy-done.1, f32[4,32,1024]{2,1,0:T(8,128)S(1)} %get-tuple-element.27.u_in, f32[4,32,1024]{2,1,0:T(8,128)S(1)} %get-tuple-element.28.q_in, f32[4,32,1024]{2,1,0:T(8,128)S(1)} %get-tuple-element.29.z_in), custom_call_target="tpu_custom_call" | custom-call | tf_op jit(solution)/shard_map/update/pallas_call | solution.py:395
Async XLA Ops:
  0.6 1.0 %copy-start = (f32[4,32,1024]{2,1,0:T(8,128)S(1)}, f32[4,32,1024]{2,1,0:T(8,128)}, u32[]{:S(2)}) copy-start(f32[4,32,1024]{2,1,0:T(8,128)} %latent.3) | copy-start | bytes 1572868
  1.7 1.0 %copy-start.2 = (s32[4,32,1024]{2,1,0:T(8,128)S(1)}, s32[4,32,1024]{2,1,0:T(8,128)}, u32[]{:S(2)}) copy-start(s32[4,32,1024]{2,1,0:T(8,128)} %counts.1) | copy-start | bytes 1572868
  2.7 1.0 %copy-start.3 = (f32[4,32,1024]{2,1,0:T(8,128)S(1)}, f32[4,32,1024]{2,1,0:T(8,128)}, u32[]{:S(2)}) copy-start(f32[4,32,1024]{2,1,0:T(8,128)} %exposure.1) | copy-start | bytes 1572868
  3.8 0.7 copy-start.4
  4.4 0.7 copy-start.5
  7.4 7.0 %collective-permute-start = (f32[48,1024]{1,0:T(8,128)S(1)}, f32[48,1024]{1,0:T(8,128)S(1)}, u32[]{:S(2)}, u32[]{:S(2)}) collective-permute-start(f32[48,1024]{1,0:T(8,128)S(1)} %get-tuple-element.19), channel_id=1, source_target_pairs={{0,1},{1,2},{2,3},{3,4},{4,5},{5,6},{6,7},{7,8},{8,9},{9,10},{10,1... | collective-permute-start | bytes 589832 | tf_op jit(solution)/shard_map/ppermute | solution.py:357
  11.8 6.6 %collective-permute-start.1 = (f32[48,1024]{1,0:T(8,128)S(1)}, f32[48,1024]{1,0:T(8,128)S(1)}, u32[]{:S(2)}, u32[]{:S(2)}) collective-permute-start(f32[48,1024]{1,0:T(8,128)S(1)} %get-tuple-element.20), channel_id=1, source_target_pairs={{1,0},{2,1},{3,2},{4,3},{5,4},{6,5},{7,6},{8,7},{9,8},{10,9},{11,1... | collective-permute-start | bytes 589832 | tf_op jit(solution)/shard_map/ppermute | solution.py:358
  19.8 13.8 %collective-permute-start.2 = (f32[152,1024]{1,0:T(8,128)S(1)}, f32[152,1024]{1,0:T(8,128)S(1)}, u32[]{:S(2)}, u32[]{:S(2)}) collective-permute-start(f32[152,1024]{1,0:T(8,128)S(1)} %get-tuple-element.24), channel_id=1, source_target_pairs={{16,32},{32,16},{48,64},{64,48},{80,96},{96,80},{112,128},{128,112... | collective-permute-start | bytes 1867784 | tf_op jit(solution)/shard_map/ppermute | solution.py:372
  25.7 7.9 %collective-permute-start.3 = (f32[152,1024]{1,0:T(8,128)S(1)}, f32[152,1024]{1,0:T(8,128)S(1)}, u32[]{:S(2)}, u32[]{:S(2)}) collective-permute-start(f32[152,1024]{1,0:T(8,128)S(1)} %get-tuple-element.25), channel_id=1, source_target_pairs={{0,16},{16,0},{32,48},{48,32},{64,80},{80,64},{96,112},{112,96},{1... | collective-permute-start | bytes 1867784 | tf_op jit(solution)/shard_map/ppermute | solution.py:373
  36.2 43.3 %copy-start.1 = (f32[4,32,1024]{2,1,0:T(8,128)S(1)}, f32[4,32,1024]{2,1,0:T(8,128)}, u32[]{:S(2)}) copy-start(f32[4,32,1024]{2,1,0:T(8,128)} %latent.3) | copy-start | bytes 1572868

commit v4 on v3

--- a/solution.py
+++ b/solution.py
@@ -28,6 +28,7 @@
 VMEM = pl.BlockSpec(memory_space=pltpu.VMEM)
 HBM = pl.BlockSpec(memory_space=pltpu.HBM)
 PARAMS = pltpu.CompilerParams(vmem_limit_bytes=40 * 1024 * 1024)
+FETCHING = pltpu.CompilerParams(vmem_limit_bytes=53000 * 1024)
 
 
 def f32(*shape):
@@ -88,12 +89,8 @@
 
 
 def intensity_kernel(
-    ids_in, coef_in, latent, counts, exposure, lat, exc, inten, head, tail, ids, coef, cnt, exposed, sems
+    offset, latent, counts, exposure, lat, exc, inten, head, tail, cnt, exposed, sems
 ):
-    small = [
-        pltpu.make_async_copy(ids_in, ids, sems.at[3 * DAYS]),
-        pltpu.make_async_copy(coef_in, coef, sems.at[3 * DAYS + 1]),
-    ]
     days = [
         (
             pltpu.make_async_copy(latent.at[t], lat.at[t], sems.at[3 * t]),
@@ -102,18 +99,12 @@
         )
         for t in range(DAYS)
     ]
-    for copy in small:
-        copy.start()
     for copies in days:
         for copy in copies:
             copy.start()
-    for copy in small:
-        copy.wait()
     row = row_iota()
-    blocks = 8 // REGION_ROWS
     offsets = [
-        jnp.where(row < REGION_ROWS, coef[ids[blocks * i]], coef[ids[blocks * i + 1]])
-        for i in range(OWN // 8)
+        jnp.concatenate([offset[rows(i), :]] * (COLUMNS // 128), axis=1) for i in range(OWN // 8)
     ]
     for t in range(DAYS):
         for copy in days[t]:
@@ -302,26 +293,30 @@
     write_sets(sets, recentred(got))
 
 
-def update_kernel(got, latent, u_in, q_in, z_in, updated, residual, factors):
-    @pl.when(pl.program_id(0) == 0)
-    def _():
-        m0, _, ww, _, wy, centre = recentred(got)
-        alpha0 = 1.0 / centre
-        norm1 = alpha0 * alpha0 * ww
-        beta = norm1 / m0
-        curvature1 = alpha0 * alpha0 * wy - beta * beta * (centre * m0)
-        factors[0:1, :] = alpha0
-        factors[1:2, :] = beta
-        factors[2:3, :] = norm1 / curvature1
-
-    alpha0, beta, alpha1 = (factors[k : k + 1, 0:1] for k in range(3))
-    for i in range(OWN // 8):
-        u, q, z = u_in[0, rows(i), :], q_in[0, rows(i), :], z_in[0, rows(i), :]
-        residual1 = u - alpha0 * q
-        direction1 = residual1 + beta * u
-        image1 = (q - alpha0 * z) + beta * q
-        updated[0, rows(i), :] = latent[0, rows(i), :] + (alpha0 * u + alpha1 * direction1)
-        residual[0, rows(i), :] = residual1 - alpha1 * image1
+def update_kernel(got, latent, u_in, q_in, z_in, updated, residual, new, left, sems):
+    m0, _, ww, _, wy, centre = (v[:, :1] for v in recentred(got))
+    alpha0 = 1.0 / centre
+    norm1 = alpha0 * alpha0 * ww
+    beta = norm1 / m0
+    curvature1 = alpha0 * alpha0 * wy - beta * beta * (centre * m0)
+    alpha1 = norm1 / curvature1
+    copies = []
+    for t in range(DAYS):
+        for i in range(OWN // 8):
+            u, q, z = u_in[t, rows(i), :], q_in[t, rows(i), :], z_in[t, rows(i), :]
+            residual1 = u - alpha0 * q
+            direction1 = residual1 + beta * u
+            image1 = (q - alpha0 * z) + beta * q
+            new[t, rows(i), :] = latent[t, rows(i), :] + (alpha0 * u + alpha1 * direction1)
+            left[t, rows(i), :] = residual1 - alpha1 * image1
+        copies += [
+            pltpu.make_async_copy(new.at[t], updated.at[t], sems.at[2 * t]),
+            pltpu.make_async_copy(left.at[t], residual.at[t], sems.at[2 * t + 1]),
+        ]
+        copies[-2].start()
+        copies[-1].start()
+    for copy in copies:
+        copy.wait()
 
 
 def gathered(sets, axis):
@@ -338,21 +333,24 @@
     def vmem(shape, dtype=jnp.float32):
         return pltpu.VMEM(shape, dtype)
 
+    region = jnp.repeat(region_ids, REGION_ROWS)
+    one_hot = region[:, None] == jnp.arange(coefficients.shape[0])[None, :]
+    offset = jnp.sum(jnp.where(one_hot, coefficients[None, :], 0.0), axis=1)
+    offset = jnp.broadcast_to(offset[:, None], (OWN, 128))
+
     lat, exc, inten, head, tail = pl.pallas_call(
         intensity_kernel,
         out_shape=(field, field, field, edge, edge),
-        in_specs=[HBM] * 5,
+        in_specs=[VMEM] + [HBM] * 3,
         out_specs=(VMEM,) * 5,
         scratch_shapes=[
-            pltpu.SMEM(region_ids.shape, jnp.int32),
-            pltpu.SMEM(coefficients.shape, jnp.float32),
             vmem(counts.shape, jnp.int32),
             vmem(exposure.shape),
-            pltpu.SemaphoreType.DMA((3 * DAYS + 2,)),
+            pltpu.SemaphoreType.DMA((3 * DAYS,)),
         ],
-        compiler_params=PARAMS,
+        compiler_params=FETCHING,
         name="intensity",
-    )(region_ids, coefficients, latent, counts, exposure)
+    )(offset, latent, counts, exposure)
 
     above = lax.ppermute(tail, "space", [(i, i + 1) for i in range(spaces - 1)])
     below = lax.ppermute(head, "space", [(i + 1, i) for i in range(spaces - 1)])
@@ -388,17 +386,20 @@
         out_shape=f32(8 * spaces, 128),
         in_specs=[VMEM],
         out_specs=VMEM,
+        compiler_params=PARAMS,
         name="regroup",
     )(gathered(sets, "tm"))
 
-    day = pl.BlockSpec((1, OWN, COLUMNS), lambda t: (t, 0, 0))
     return pl.pallas_call(
         update_kernel,
-        grid=(DAYS,),
         out_shape=(field, field),
-        in_specs=[pl.BlockSpec((8 * spaces, 128), lambda t: (0, 0)), day, day, day, day],
-        out_specs=(day, day),
-        scratch_shapes=[vmem((8, 128))],
+        in_specs=[VMEM] * 5,
+        out_specs=(HBM, HBM),
+        scratch_shapes=[
+            vmem(latent.shape),
+            vmem(latent.shape),
+            pltpu.SemaphoreType.DMA((2 * DAYS,)),
+        ],
         compiler_params=PARAMS,
         name="update",
     )(gathered(sets, "space"), latent, u, q, z)

time: 81.8 us -> 75.7 us (0.925)
  local copies, waits for them, and re-layouts: 4.43 us -> 1.46 us
  Pallas kernels: 9.69 us -> 6.93 us
    unnamed x12 -> x4, local copies, waits for them, and re-layouts: 4.43 us -> 0.58 us
    pallas_call x1, Pallas kernels: 1.58 us -> 0.05 us  [body(): pl.pallas_call(regroup_kernel, out_shape=f32(8 * spaces, 128), in_specs=[...]
where the time goes in v4:
time: 75.7 us; the launch traced here: 75.4 us
  blocking collectives  41.4 us (55%)
  starting transfers between devices  13.5 us (18%)
  waiting for transfers between devices  11.3 us (15%)
  Pallas kernels  6.93 us (9%)
  local copies, waits for them, and re-layouts  1.46 us (2%)
    all_to_all x2, blocking collectives, gathered(): got = lax.all_to_all(sets.reshape(count, 8, 128), axis, 0, 0)  41.4 us
    ppermute x1, waiting for transfers between devices, body(): y_got = lax.ppermute(y_msg, 'tm', across)  5.97 us
    ppermute x1, starting transfers between devices, body(): y_got = lax.ppermute(y_msg, 'tm', across)  5.89 us
    ppermute x1, starting transfers between devices, body(): above = lax.ppermute(tail, 'space', [(i, i + 1) for i in range(spaces - 1)])  4.38 us
    ppermute x1, waiting for transfers between devices, body(): below = lax.ppermute(head, 'space', [(i + 1, i) for i in range(spaces - 1)])  4 us
    pallas_call x1, Pallas kernels, body(): pl.pallas_call(image_kernel, out_shape=(field, field, field, f32(8 * time...  2.67 us
    ppermute x1, starting transfers between devices, body(): c_got = lax.ppermute(c_msg, 'tm', within)  1.92 us
    pallas_call x1, Pallas kernels, body(): pl.pallas_call(intensity_kernel, out_shape=(field, field, field, edge, ed...  1.62 us
  transfers between devices with their start and end apart: 4, of which 3 were waited for; matrix products, arithmetic and copies ran while one was open for 0% of the time, Pallas kernels for 0%

profile of v4, /device:TPU:1, one launch (start us, length us, event | category | flops | bytes accessed | tf_op | source)
XLA Modules:
  0.0 75.4 jit_solution(13971858238021160105)
XLA Ops:
  0.6 0.7 broadcast_in_dim.23
  1.4 0.0 copy-start.1
  1.4 0.1 eq.15
  1.4 0.6 copy-done.1
  2.0 0.1 select_reduce_fusion
  2.1 0.1 broadcast_in_dim.26.offset
  2.2 1.6 %intensity.1 = (f32[4,32,1024]{2,1,0:T(8,128)S(1)}, f32[4,32,1024]{2,1,0:T(8,128)S(1)}, f32[4,32,1024]{2,1,0:T(8,128)S(1)}, f32[48,1024]{1,0:T(8,128)S(1)}, f32[48,1024]{1,0:T(8,128)S(1)}) custom-call(f32[32,128]{1,0:T(8,128)S(1)} %broadcast_in_dim.26.offset, f32[4,32,1024]{2,1,0:T(8,128)} %latent.3, s32[4,32,1024]{2,1,0:T(8,128)} %counts.1, ...), custom_call_target="tpu_custom_call" | custom-call | tf_op jit(solution)/shard_map/intensity/pallas_call | solution.py:341
  3.8 4.4 %collective-permute-start = (f32[48,1024]{1,0:T(8,128)S(1)}, f32[48,1024]{1,0:T(8,128)S(1)}, u32[]{:S(2)}, u32[]{:S(2)}) collective-permute-start(f32[48,1024]{1,0:T(8,128)S(1)} %get-tuple-element.19), channel_id=1, source_target_pairs={{0,1},{1,2},{2,3},{3,4},{4,5},{5,6},{6,7},{7,8},{8,9},{9,10},{10,1... | collective-permute-start | bytes 589832 | tf_op jit(solution)/shard_map/ppermute | solution.py:355
  8.2 1.3 %collective-permute-start.1 = (f32[48,1024]{1,0:T(8,128)S(1)}, f32[48,1024]{1,0:T(8,128)S(1)}, u32[]{:S(2)}, u32[]{:S(2)}) collective-permute-start(f32[48,1024]{1,0:T(8,128)S(1)} %get-tuple-element.20), channel_id=1, source_target_pairs={{1,0},{2,1},{3,2},{4,3},{5,4},{6,5},{7,6},{8,7},{9,8},{10,9},{11,1... | collective-permute-start | bytes 589832 | tf_op jit(solution)/shard_map/ppermute | solution.py:356
  9.5 1.3 %collective-permute-done.above = f32[48,1024]{1,0:T(8,128)S(1)} collective-permute-done((f32[48,1024]{1,0:T(8,128)S(1)}, f32[48,1024]{1,0:T(8,128)S(1)}, u32[]{:S(2)}, u32[]{:S(2)}) %collective-permute-start) | collective-permute-done | bytes 196640 | tf_op jit(solution)/shard_map/ppermute | solution.py:355
  10.8 4.0 %collective-permute-done.1.below = f32[48,1024]{1,0:T(8,128)S(1)} collective-permute-done((f32[48,1024]{1,0:T(8,128)S(1)}, f32[48,1024]{1,0:T(8,128)S(1)}, u32[]{:S(2)}, u32[]{:S(2)}) %collective-permute-start.1) | collective-permute-done | bytes 196640 | tf_op jit(solution)/shard_map/ppermute | solution.py:356
  14.8 1.4 %residual.1 = (f32[4,48,1024]{2,1,0:T(8,128)S(1)}, f32[4,48,1024]{2,1,0:T(8,128)S(1)}, f32[2,48,1024]{2,1,0:T(8,128)S(1)}, f32[152,1024]{1,0:T(8,128)S(1)}, f32[152,1024]{1,0:T(8,128)S(1)}) custom-call(f32[4,32,1024]{2,1,0:T(8,128)S(1)} %get-tuple-element.16.latent, f32[4,32,1024]{2,1,0:T(8,128)S(1)} %get-tuple-element.17.inten, ...), custom_call_target="tpu_custom_call" | custom-call | tf_op jit(solution)/shard_map/residual/pallas_call | solution.py:358
  16.2 5.9 %collective-permute-start.2 = (f32[152,1024]{1,0:T(8,128)S(1)}, f32[152,1024]{1,0:T(8,128)S(1)}, u32[]{:S(2)}, u32[]{:S(2)}) collective-permute-start(f32[152,1024]{1,0:T(8,128)S(1)} %get-tuple-element.24), channel_id=1, source_target_pairs={{16,32},{32,16},{48,64},{64,48},{80,96},{96,80},{112,128},{128,112... | collective-permute-start | bytes 1867784 | tf_op jit(solution)/shard_map/ppermute | solution.py:370
  22.1 1.9 %collective-permute-start.3 = (f32[152,1024]{1,0:T(8,128)S(1)}, f32[152,1024]{1,0:T(8,128)S(1)}, u32[]{:S(2)}, u32[]{:S(2)}) collective-permute-start(f32[152,1024]{1,0:T(8,128)S(1)} %get-tuple-element.25), channel_id=1, source_target_pairs={{0,16},{16,0},{32,48},{48,32},{64,80},{80,64},{96,112},{112,96},{1... | collective-permute-start | bytes 1867784 | tf_op jit(solution)/shard_map/ppermute | solution.py:371
  24.0 6.0 %collective-permute-done.2.y_msg = f32[152,1024]{1,0:T(8,128)S(1)} collective-permute-done((f32[152,1024]{1,0:T(8,128)S(1)}, f32[152,1024]{1,0:T(8,128)S(1)}, u32[]{:S(2)}, u32[]{:S(2)}) %collective-permute-start.2) | collective-permute-done | bytes 622624 | tf_op jit(solution)/shard_map/ppermute | solution.py:370
  30.0 0.0 collective-permute-done.3.c_msg
  30.0 2.7 %image.1 = (f32[4,32,1024]{2,1,0:T(8,128)S(1)}, f32[4,32,1024]{2,1,0:T(8,128)S(1)}, f32[4,32,1024]{2,1,0:T(8,128)S(1)}, f32[256,128]{1,0:T(8,128)S(1)}) custom-call(f32[4,48,1024]{2,1,0:T(8,128)S(1)} %get-tuple-element.21.res, f32[2,48,1024]{2,1,0:T(8,128)S(1)} %get-tuple-element.22.inner, f32[4,48,1024]{2,1,0:T(8,128)S(1)} %get-tuple-element.23.lat, ...), custom_call_target="tpu_custom_call" | custom-call | tf_op jit(solution)/shard_map/image/pallas_call | solution.py:374
  32.7 0.0 copy-start
  32.7 15.6 %all_to_all.10 = f32[32,8,128]{2,1,0:T(8,128)S(1)} all-to-all(f32[32,8,128]{2,1,0:T(8,128)S(1)} %bitcast.7), channel_id=1, replica_groups=mesh['tm'=32,'space'=16] {'tm'}, dimensions={0} | all-to-all | bytes 262144 | tf_op jit(solution)/shard_map/all_to_all | solution.py:324
  48.4 25.8 %all_to_all.11 = f32[16,8,128]{2,1,0:T(8,128)S(1)} all-to-all(f32[16,8,128]{2,1,0:T(8,128)S(1)} %bitcast.6), channel_id=1, replica_groups=mesh['tm'=32,'space'=16] {'space'}, dimensions={0} | all-to-all | bytes 131072 | tf_op jit(solution)/shard_map/all_to_all | solution.py:324
  74.2 0.0 copy-done
  74.2 1.2 %update.1 = (f32[4,32,1024]{2,1,0:T(8,128)}, f32[4,32,1024]{2,1,0:T(8,128)}) custom-call(f32[128,128]{1,0:T(8,128)S(1)} %bitcast.5, f32[4,32,1024]{2,1,0:T(8,128)S(1)} %copy-done, f32[4,32,1024]{2,1,0:T(8,128)S(1)} %get-tuple-element.27.u_in, f32[4,32,1024]{2,1,0:T(8,128)S(1)} %get-tuple-element.28.q_in, f32[4,32,1024]{2,1,0:T(8,128)S(1)} %get-tuple-element.29.z_in), custom_call_target="tpu_custom_call" | custom-call | tf_op jit(solution)/shard_map/update/pallas_call | solution.py:393
  (1 shorter events, 0.0 us)
Async XLA Ops:
  1.4 0.7 copy-start.1
  3.8 7.0 %collective-permute-start = (f32[48,1024]{1,0:T(8,128)S(1)}, f32[48,1024]{1,0:T(8,128)S(1)}, u32[]{:S(2)}, u32[]{:S(2)}) collective-permute-start(f32[48,1024]{1,0:T(8,128)S(1)} %get-tuple-element.19), channel_id=1, source_target_pairs={{0,1},{1,2},{2,3},{3,4},{4,5},{5,6},{6,7},{7,8},{8,9},{9,10},{10,1... | collective-permute-start | bytes 589832 | tf_op jit(solution)/shard_map/ppermute | solution.py:355
  8.2 6.6 %collective-permute-start.1 = (f32[48,1024]{1,0:T(8,128)S(1)}, f32[48,1024]{1,0:T(8,128)S(1)}, u32[]{:S(2)}, u32[]{:S(2)}) collective-permute-start(f32[48,1024]{1,0:T(8,128)S(1)} %get-tuple-element.20), channel_id=1, source_target_pairs={{1,0},{2,1},{3,2},{4,3},{5,4},{6,5},{7,6},{8,7},{9,8},{10,9},{11,1... | collective-permute-start | bytes 589832 | tf_op jit(solution)/shard_map/ppermute | solution.py:356
  16.2 13.8 %collective-permute-start.2 = (f32[152,1024]{1,0:T(8,128)S(1)}, f32[152,1024]{1,0:T(8,128)S(1)}, u32[]{:S(2)}, u32[]{:S(2)}) collective-permute-start(f32[152,1024]{1,0:T(8,128)S(1)} %get-tuple-element.24), channel_id=1, source_target_pairs={{16,32},{32,16},{48,64},{64,48},{80,96},{96,80},{112,128},{128,112... | collective-permute-start | bytes 1867784 | tf_op jit(solution)/shard_map/ppermute | solution.py:370
  22.1 7.9 %collective-permute-start.3 = (f32[152,1024]{1,0:T(8,128)S(1)}, f32[152,1024]{1,0:T(8,128)S(1)}, u32[]{:S(2)}, u32[]{:S(2)}) collective-permute-start(f32[152,1024]{1,0:T(8,128)S(1)} %get-tuple-element.25), channel_id=1, source_target_pairs={{0,16},{16,0},{32,48},{48,32},{64,80},{80,64},{96,112},{112,96},{1... | collective-permute-start | bytes 1867784 | tf_op jit(solution)/shard_map/ppermute | solution.py:371
  32.7 41.5 %copy-start = (f32[4,32,1024]{2,1,0:T(8,128)S(1)}, f32[4,32,1024]{2,1,0:T(8,128)}, u32[]{:S(2)}) copy-start(f32[4,32,1024]{2,1,0:T(8,128)} %latent.3) | copy-start | bytes 1572868

commit v5 on v4

--- a/solution.py
+++ b/solution.py
@@ -55,6 +55,22 @@
 
 def framed(ref):
     return lambda s, i: ref[s, rows(i), :]
+
+
+class Either:
+    def __init__(self, which, first, second):
+        self.which, self.first, self.second = which, first, second
+
+    def __getitem__(self, at):
+        return jnp.where(self.which, self.first[at], self.second[at])
+
+
+def alike():
+    return lax.rem(lax.axis_index("space") + lax.axis_index("tm"), 2) == 0
+
+
+def edges(first, second):
+    return Either(alike(), second, first), Either(alike(), first, second)
 
 
 def apply_k(load, dst, planes, has_above, has_below, tiles=range(TILES)):
@@ -89,8 +105,14 @@
 
 
 def intensity_kernel(
-    offset, latent, counts, exposure, lat, exc, inten, head, tail, cnt, exposed, sems
+    offset, latent, counts, exposure, lat, exc, inten, z_first, z_second, cnt, exposed, sems
 ):
+    same = alike()
+
+    def send(at, tail, head):
+        z_first[rows(at), :] = jnp.where(same, tail, head)
+        z_second[rows(at), :] = jnp.where(same, head, tail)
+
     days = [
         (
             pltpu.make_async_copy(latent.at[t], lat.at[t], sems.at[3 * t]),
@@ -103,9 +125,12 @@
         for copy in copies:
             copy.start()
     row = row_iota()
-    offsets = [
-        jnp.concatenate([offset[rows(i), :]] * (COLUMNS // 128), axis=1) for i in range(OWN // 8)
-    ]
+    blocks = 8 // REGION_ROWS
+    offsets = []
+    for i in range(OWN // 8):
+        first, second = (offset[blocks * i + k : blocks * i + k + 1, :] for k in range(blocks))
+        tile = jnp.where(row[:, :128] < REGION_ROWS, first, second)
+        offsets.append(jnp.concatenate([tile] * (COLUMNS // 128), axis=1))
     for t in range(DAYS):
         for copy in days[t]:
             copy.wait()
@@ -115,18 +140,23 @@
             exc[t, rows(i), :] = value - cnt[t, rows(i), :].astype(jnp.float32)
     last = OWN // 8 - 1
     for t in range(DAYS):
-        tail[rows(t), :] = jnp.where(row < 2, up_roll(inten[t, rows(last), :], 2), lat[t, rows(last), :])
-        head[rows(t), :] = jnp.where(row >= 6, up_roll(inten[t, rows(0), :], 6), lat[t, rows(0), :])
+        send(
+            t,
+            jnp.where(row < 2, up_roll(inten[t, rows(last), :], 2), lat[t, rows(last), :]),
+            jnp.where(row >= 6, up_roll(inten[t, rows(0), :], 6), lat[t, rows(0), :]),
+        )
     for k in range(DAYS // 2):
         a, b = 2 * k, 2 * k + 1
-        tail[rows(DAYS + k), :] = jnp.where(
-            row >= 4, exc[a, rows(last), :], up_roll(exc[b, rows(last), :], 4)
+        send(
+            DAYS + k,
+            jnp.where(row >= 4, exc[a, rows(last), :], up_roll(exc[b, rows(last), :], 4)),
+            jnp.where(row < 4, exc[a, rows(0), :], up_roll(exc[b, rows(0), :], 4)),
         )
-        head[rows(DAYS + k), :] = jnp.where(row < 4, exc[a, rows(0), :], up_roll(exc[b, rows(0), :], 4))
-
-
-def residual_kernel(latent, inten, exc, above, below, lat, res, inner, y_msg, c_msg, tmp):
+
+
+def residual_kernel(latent, inten, exc, z_first, z_second, lat, res, inner, y_msg, c_msg, tmp):
     has_above, has_below, has_before, has_after, even = places()
+    above, below = edges(z_first, z_second)
     row = row_iota()
 
     def field(t, i):
@@ -182,9 +212,10 @@
 
 
 def image_kernel(
-    res, inner, lat, inten, above, below, y_msg, c_msg, u_out, q_out, z_out, sets, r6, q6, f6, tmp
+    res, inner, lat, inten, z_first, z_second, y_msg, c_msg, u_out, q_out, z_out, sets, r6, mixed, f6, tmp
 ):
     has_above, has_below, has_before, has_after, even = places()
+    above, below = edges(z_first, z_second)
     weight = day_weights(has_before, has_after)
     last = DAYS + 1
 
@@ -218,10 +249,6 @@
             for t in range(DAYS + 2)
         ]
         r = [residual(t, i) for t in range(DAYS + 2)]
-        for t in range(DAYS):
-            q6[t + 1, rows(i), :] = (
-                weight[t] * f[t + 1] - COUPLE * (f[t] + f[t + 2]) + intensity(t, i) * r[t + 1]
-            )
         if i in OWN_TILES:
             q_side, i_side = got(Q_AT + i - 1), got(I_AT + i - 1)
         else:
@@ -229,21 +256,24 @@
             i_side = [up_roll(v, 4) for v in q_side]
         before = INNER * f[0] - COUPLE * f[1] + q_side[0] + i_side[0] * r[0]
         after = INNER * f[last] - COUPLE * f[DAYS] + q_side[1] + i_side[1] * r[last]
-        q6[0, rows(i), :] = jnp.where(has_before, before, 0.0)
-        q6[last, rows(i), :] = jnp.where(has_after, after, 0.0)
-    every = [(t, t) for t in range(DAYS + 2)]
-    apply_k(framed(q6), tmp, every, has_above, has_below)
-    apply_k(framed(tmp), f6, every, has_above, has_below, OWN_TILES)
+        q = [jnp.where(has_before, before, 0.0)]
+        for t in range(DAYS):
+            q.append(weight[t] * f[t + 1] - COUPLE * (f[t] + f[t + 2]) + intensity(t, i) * r[t + 1])
+        q.append(jnp.where(has_after, after, 0.0))
+        for t in range(DAYS):
+            mixed[t, rows(i), :] = weight[t] * q[t + 1] - COUPLE * (q[t] + q[t + 2])
+            if i in OWN_TILES:
+                q_out[t, rows(i - 1), :] = q[t + 1]
+    days = [(t, t) for t in range(DAYS)]
+    apply_k(framed(mixed), tmp, days, has_above, has_below)
+    apply_k(framed(tmp), mixed, days, has_above, has_below, OWN_TILES)
     zero = jnp.zeros((8, COLUMNS), jnp.float32)
 
     uu = uq = zero
     for i in OWN_TILES:
-        f = [f6[t, rows(i), :] for t in range(DAYS + 2)]
         for t in range(DAYS):
-            q, u = q6[t + 1, rows(i), :], residual(t + 1, i)
-            z = weight[t] * f[t + 1] - COUPLE * (f[t] + f[t + 2]) + intensity(t, i) * q
-            z_out[t, rows(i - 1), :] = z
-            q_out[t, rows(i - 1), :] = q
+            q, u = q_out[t, rows(i - 1), :], residual(t + 1, i)
+            z_out[t, rows(i - 1), :] = mixed[t, rows(i), :] + intensity(t, i) * q
             u_out[t, rows(i - 1), :] = u
             uu = uu + u * u
             uq = uq + u * q
@@ -333,12 +363,11 @@
     def vmem(shape, dtype=jnp.float32):
         return pltpu.VMEM(shape, dtype)
 
-    region = jnp.repeat(region_ids, REGION_ROWS)
-    one_hot = region[:, None] == jnp.arange(coefficients.shape[0])[None, :]
-    offset = jnp.sum(jnp.where(one_hot, coefficients[None, :], 0.0), axis=1)
-    offset = jnp.broadcast_to(offset[:, None], (OWN, 128))
-
-    lat, exc, inten, head, tail = pl.pallas_call(
+    one_hot = region_ids[:, None, None] == jnp.arange(coefficients.shape[0])[None, :, None]
+    offset = jnp.where(one_hot, coefficients[None, :, None], 0.0)
+    offset = jnp.sum(jnp.broadcast_to(offset, offset.shape[:2] + (128,)), axis=1)
+
+    lat, exc, inten, z_first, z_second = pl.pallas_call(
         intensity_kernel,
         out_shape=(field, field, field, edge, edge),
         in_specs=[VMEM] + [HBM] * 3,
@@ -352,8 +381,18 @@
         name="intensity",
     )(offset, latent, counts, exposure)
 
-    above = lax.ppermute(tail, "space", [(i, i + 1) for i in range(spaces - 1)])
-    below = lax.ppermute(head, "space", [(i + 1, i) for i in range(spaces - 1)])
+    def pairs(count, first):
+        return [p for i in range(first, count - 1, 2) for p in ((i, i + 1), (i + 1, i))]
+
+    def turns(k):
+        return [
+            (t * spaces + i, t * spaces + j)
+            for t in range(times)
+            for i, j in pairs(spaces, (t + k) % 2)
+        ]
+
+    z_first = lax.ppermute(z_first, ("tm", "space"), turns(0))
+    z_second = lax.ppermute(z_second, ("tm", "space"), turns(1))
 
     spatial, res, inner, y_msg, c_msg = pl.pallas_call(
         residual_kernel,
@@ -363,12 +402,10 @@
         scratch_shapes=[vmem(four.shape)],
         compiler_params=PARAMS,
         name="residual",
-    )(lat, inten, exc, above, below)
-
-    across = [p for i in range(1, times - 1, 2) for p in ((i, i + 1), (i + 1, i))]
-    within = [p for i in range(0, times - 1, 2) for p in ((i, i + 1), (i + 1, i))]
-    y_got = lax.ppermute(y_msg, "tm", across)
-    c_got = lax.ppermute(c_msg, "tm", within)
+    )(lat, inten, exc, z_first, z_second)
+
+    y_got = lax.ppermute(y_msg, "tm", pairs(times, 1))
+    c_got = lax.ppermute(c_msg, "tm", pairs(times, 0))
 
     six = vmem((DAYS + 2, FRAME, COLUMNS))
     u, q, z, sets = pl.pallas_call(
@@ -379,7 +416,7 @@
         scratch_shapes=[six] * 4,
         compiler_params=PARAMS,
         name="image",
-    )(res, inner, spatial, inten, above, below, y_got, c_got)
+    )(res, inner, spatial, inten, z_first, z_second, y_got, c_got)
 
     sets = pl.pallas_call(
         regroup_kernel,

time: 75.7 us -> 74.4 us (0.983)
  waiting for transfers between devices: 11.3 us -> 9.69 us
  local copies, waits for them, and re-layouts: 1.46 us -> 0.08 us
  blocking collectives: 41.4 us -> 42.7 us
  other arithmetic: 0.09 us -> 0.85 us
    ppermute x4, waiting for transfers between devices: 11.3 us -> 9.69 us  [the longest x1 6.06 us: body(): y_got = lax.ppermute(y_msg, 'tm', pairs(times, 1))]
    all_to_all x2, blocking collectives: 41.4 us -> 42.7 us  [gathered(): got = lax.all_to_all(sets.reshape(count, 8, 128), axis, 0, 0)]
    broadcast_in_dim x2 -> x0, local copies, waits for them, and re-layouts: 0.8 us -> none  [the longest x1 0.72 us: body(): region = jnp.repeat(region_ids, REGION_ROWS)]
    reduce_sum x1, other arithmetic: 0.09 us -> 0.85 us  [body(): jnp.sum(jnp.broadcast_to(offset, offset.shape[:2] + (128,)), axis=1)]
  transfers between devices with their start and end apart: 4 -> 4, of which waited for: 3 -> 2; matrix products, arithmetic and copies ran while one was open for 0% -> 0% of each run, Pallas kernels for 0% -> 0%
where the time goes in v5:
time: 74.4 us; the launch traced here: 74.1 us
  blocking collectives  42.7 us (57%)
  starting transfers between devices  13.4 us (18%)
  waiting for transfers between devices  9.69 us (13%)
  Pallas kernels  6.67 us (9%)
  other arithmetic  0.85 us (1%)
    all_to_all x2, blocking collectives, gathered(): got = lax.all_to_all(sets.reshape(count, 8, 128), axis, 0, 0)  42.7 us
    ppermute x1, starting transfers between devices, body(): z_second = lax.ppermute(z_second, ('tm', 'space'), turns(1))  7.25 us
    ppermute x1, waiting for transfers between devices, body(): y_got = lax.ppermute(y_msg, 'tm', pairs(times, 1))  6.06 us
    ppermute x1, waiting for transfers between devices, body(): z_second = lax.ppermute(z_second, ('tm', 'space'), turns(1))  3.63 us
    ppermute x1, starting transfers between devices, body(): c_got = lax.ppermute(c_msg, 'tm', pairs(times, 0))  3.56 us
    pallas_call x1, Pallas kernels, body(): pl.pallas_call(image_kernel, out_shape=(field, field, field, f32(8 * time...  2.36 us
    ppermute x1, starting transfers between devices, body(): y_got = lax.ppermute(y_msg, 'tm', pairs(times, 1))  1.92 us
    pallas_call x1, Pallas kernels, body(): pl.pallas_call(intensity_kernel, out_shape=(field, field, field, edge, ed...  1.62 us
  transfers between devices with their start and end apart: 4, of which 2 were waited for; matrix products, arithmetic and copies ran while one was open for 0% of the time, Pallas kernels for 0%

profile of v5, /device:TPU:1, one launch (start us, length us, event | category | flops | bytes accessed | tf_op | source)
XLA Modules:
  0.0 74.1 jit_solution(1269600990953333645)
XLA Ops:
  0.6 0.9 %select_reduce_fusion = f32[8]{0:T(128)S(1)} fusion(f32[16]{0:T(128)} %param.9, s32[8]{0:T(128)} %param.8), kind=kLoop, calls=%fused_computation | loop fusion | flops 376 | bytes 128 | tf_op jit(solution)/shard_map/reduce_sum | solution.py:368
  1.5 0.1 reduce_sum.12.offset
  1.6 1.6 %intensity.1 = (f32[4,32,1024]{2,1,0:T(8,128)S(1)}, f32[4,32,1024]{2,1,0:T(8,128)S(1)}, f32[4,32,1024]{2,1,0:T(8,128)S(1)}, f32[48,1024]{1,0:T(8,128)S(1)}, f32[48,1024]{1,0:T(8,128)S(1)}) custom-call(f32[8,128]{1,0:T(8,128)S(1)} %reduce_sum.12.offset, f32[4,32,1024]{2,1,0:T(8,128)} %latent.3, s32[4,32,1024]{2,1,0:T(8,128)} %counts.1, f32[4,32,1024]{2,1,0:T(8,128)} %exposure.1), custom_call_target="tpu_custom_call" | custom-call | tf_op jit(solution)/shard_map/intensity/pallas_call | solution.py:370
  3.2 0.7 collective-permute-start
  3.9 7.2 %collective-permute-start.1 = (f32[48,1024]{1,0:T(8,128)S(1)}, f32[48,1024]{1,0:T(8,128)S(1)}, u32[]{:S(2)}, u32[]{:S(2)}) collective-permute-start(f32[48,1024]{1,0:T(8,128)S(1)} %get-tuple-element.20), channel_id=1, source_target_pairs={{1,2},{2,1},{3,4},{4,3},{5,6},{6,5},{7,8},{8,7},{9,10},{10,9},{11,... | collective-permute-start | bytes 589832 | tf_op jit(solution)/shard_map/ppermute | solution.py:395
  11.1 0.0 collective-permute-done.z_first
  11.1 3.6 %collective-permute-done.1.z_second = f32[48,1024]{1,0:T(8,128)S(1)} collective-permute-done((f32[48,1024]{1,0:T(8,128)S(1)}, f32[48,1024]{1,0:T(8,128)S(1)}, u32[]{:S(2)}, u32[]{:S(2)}) %collective-permute-start.1) | collective-permute-done | bytes 196640 | tf_op jit(solution)/shard_map/ppermute | solution.py:395
  14.8 1.5 %residual.1 = (f32[4,48,1024]{2,1,0:T(8,128)S(1)}, f32[4,48,1024]{2,1,0:T(8,128)S(1)}, f32[2,48,1024]{2,1,0:T(8,128)S(1)}, f32[152,1024]{1,0:T(8,128)S(1)}, f32[152,1024]{1,0:T(8,128)S(1)}) custom-call(f32[4,32,1024]{2,1,0:T(8,128)S(1)} %get-tuple-element.16.latent, f32[4,32,1024]{2,1,0:T(8,128)S(1)} %get-tuple-element.17.inten, ...), custom_call_target="tpu_custom_call" | custom-call | tf_op jit(solution)/shard_map/residual/pallas_call | solution.py:397
  16.2 1.9 %collective-permute-start.2 = (f32[152,1024]{1,0:T(8,128)S(1)}, f32[152,1024]{1,0:T(8,128)S(1)}, u32[]{:S(2)}, u32[]{:S(2)}) collective-permute-start(f32[152,1024]{1,0:T(8,128)S(1)} %get-tuple-element.24), channel_id=1, source_target_pairs={{16,32},{32,16},{48,64},{64,48},{80,96},{96,80},{112,128},{128,112... | collective-permute-start | bytes 1867784 | tf_op jit(solution)/shard_map/ppermute | solution.py:407
  18.2 3.6 %collective-permute-start.3 = (f32[152,1024]{1,0:T(8,128)S(1)}, f32[152,1024]{1,0:T(8,128)S(1)}, u32[]{:S(2)}, u32[]{:S(2)}) collective-permute-start(f32[152,1024]{1,0:T(8,128)S(1)} %get-tuple-element.25), channel_id=1, source_target_pairs={{0,16},{16,0},{32,48},{48,32},{64,80},{80,64},{96,112},{112,96},{1... | collective-permute-start | bytes 1867784 | tf_op jit(solution)/shard_map/ppermute | solution.py:408
  21.7 6.1 %collective-permute-done.2.y_msg = f32[152,1024]{1,0:T(8,128)S(1)} collective-permute-done((f32[152,1024]{1,0:T(8,128)S(1)}, f32[152,1024]{1,0:T(8,128)S(1)}, u32[]{:S(2)}, u32[]{:S(2)}) %collective-permute-start.2) | collective-permute-done | bytes 622624 | tf_op jit(solution)/shard_map/ppermute | solution.py:407
  27.8 0.0 collective-permute-done.3.c_msg
  27.8 2.4 %image.1 = (f32[4,32,1024]{2,1,0:T(8,128)S(1)}, f32[4,32,1024]{2,1,0:T(8,128)S(1)}, f32[4,32,1024]{2,1,0:T(8,128)S(1)}, f32[256,128]{1,0:T(8,128)S(1)}) custom-call(f32[4,48,1024]{2,1,0:T(8,128)S(1)} %get-tuple-element.21.res, f32[2,48,1024]{2,1,0:T(8,128)S(1)} %get-tuple-element.22.inner, f32[4,48,1024]{2,1,0:T(8,128)S(1)} %get-tuple-element.23.lat, ...), custom_call_target="tpu_custom_call" | custom-call | tf_op jit(solution)/shard_map/image/pallas_call | solution.py:411
  30.2 0.0 copy-start
  30.2 16.2 %all_to_all.10 = f32[32,8,128]{2,1,0:T(8,128)S(1)} all-to-all(f32[32,8,128]{2,1,0:T(8,128)S(1)} %bitcast.7), channel_id=1, replica_groups=mesh['tm'=32,'space'=16] {'tm'}, dimensions={0} | all-to-all | bytes 262144 | tf_op jit(solution)/shard_map/all_to_all | solution.py:354
  46.4 26.5 %all_to_all.11 = f32[16,8,128]{2,1,0:T(8,128)S(1)} all-to-all(f32[16,8,128]{2,1,0:T(8,128)S(1)} %bitcast.6), channel_id=1, replica_groups=mesh['tm'=32,'space'=16] {'space'}, dimensions={0} | all-to-all | bytes 131072 | tf_op jit(solution)/shard_map/all_to_all | solution.py:354
  72.9 0.0 copy-done
  72.9 1.2 %update.1 = (f32[4,32,1024]{2,1,0:T(8,128)}, f32[4,32,1024]{2,1,0:T(8,128)}) custom-call(f32[128,128]{1,0:T(8,128)S(1)} %bitcast.5, f32[4,32,1024]{2,1,0:T(8,128)S(1)} %copy-done, f32[4,32,1024]{2,1,0:T(8,128)S(1)} %get-tuple-element.27.u_in, f32[4,32,1024]{2,1,0:T(8,128)S(1)} %get-tuple-element.28.q_in, f32[4,32,1024]{2,1,0:T(8,128)S(1)} %get-tuple-element.29.z_in), custom_call_target="tpu_custom_call" | custom-call | tf_op jit(solution)/shard_map/update/pallas_call | solution.py:430
  (1 shorter events, 0.0 us)
Async XLA Ops:
  3.2 7.9 %collective-permute-start = (f32[48,1024]{1,0:T(8,128)S(1)}, f32[48,1024]{1,0:T(8,128)S(1)}, u32[]{:S(2)}, u32[]{:S(2)}) collective-permute-start(f32[48,1024]{1,0:T(8,128)S(1)} %get-tuple-element.19), channel_id=1, source_target_pairs={{0,1},{1,0},{2,3},{3,2},{4,5},{5,4},{6,7},{7,6},{8,9},{9,8},{10,11... | collective-permute-start | bytes 589832 | tf_op jit(solution)/shard_map/ppermute | solution.py:394
  3.9 10.9 %collective-permute-start.1 = (f32[48,1024]{1,0:T(8,128)S(1)}, f32[48,1024]{1,0:T(8,128)S(1)}, u32[]{:S(2)}, u32[]{:S(2)}) collective-permute-start(f32[48,1024]{1,0:T(8,128)S(1)} %get-tuple-element.20), channel_id=1, source_target_pairs={{1,2},{2,1},{3,4},{4,3},{5,6},{6,5},{7,8},{8,7},{9,10},{10,9},{11,... | collective-permute-start | bytes 589832 | tf_op jit(solution)/shard_map/ppermute | solution.py:395
  16.2 11.6 %collective-permute-start.2 = (f32[152,1024]{1,0:T(8,128)S(1)}, f32[152,1024]{1,0:T(8,128)S(1)}, u32[]{:S(2)}, u32[]{:S(2)}) collective-permute-start(f32[152,1024]{1,0:T(8,128)S(1)} %get-tuple-element.24), channel_id=1, source_target_pairs={{16,32},{32,16},{48,64},{64,48},{80,96},{96,80},{112,128},{128,112... | collective-permute-start | bytes 1867784 | tf_op jit(solution)/shard_map/ppermute | solution.py:407
  18.2 9.6 %collective-permute-start.3 = (f32[152,1024]{1,0:T(8,128)S(1)}, f32[152,1024]{1,0:T(8,128)S(1)}, u32[]{:S(2)}, u32[]{:S(2)}) collective-permute-start(f32[152,1024]{1,0:T(8,128)S(1)} %get-tuple-element.25), channel_id=1, source_target_pairs={{0,16},{16,0},{32,48},{48,32},{64,80},{80,64},{96,112},{112,96},{1... | collective-permute-start | bytes 1867784 | tf_op jit(solution)/shard_map/ppermute | solution.py:408
  30.2 42.7 %copy-start = (f32[4,32,1024]{2,1,0:T(8,128)S(1)}, f32[4,32,1024]{2,1,0:T(8,128)}, u32[]{:S(2)}) copy-start(f32[4,32,1024]{2,1,0:T(8,128)} %latent.3) | copy-start | bytes 1572868

commit v6 on v5

--- a/solution.py
+++ b/solution.py
@@ -294,20 +294,19 @@
 
 
 def write_sets(sets, values):
-    row = lax.broadcasted_iota(jnp.int32, (8, 128), 0)
-    out = jnp.zeros((8, 128), jnp.float32)
+    lane = lax.broadcasted_iota(jnp.int32, (1, 128), 1)
+    out = jnp.zeros((1, 128), jnp.float32)
     for k, value in enumerate(values):
-        out = jnp.where(row == k, value, out)
-    for n in range(sets.shape[0] // 8):
-        sets[rows(n), :] = out
+        out = jnp.where(lane == k, value, out)
+    sets[...] = jnp.broadcast_to(out, sets.shape)
 
 
 def recentred(got):
-    senders = got.shape[0] // 8
-    uu, uw, ww, uy, wy, ratio = (got[pl.ds(k, senders, 8), :] for k in range(6))
+    by_lane = got[...].T
+    uu, uw, ww, uy, wy, ratio = (by_lane[k : k + 1, :] for k in range(6))
 
     def add(v):
-        return jnp.sum(v, axis=0, keepdims=True)
+        return jnp.sum(v, axis=1, keepdims=True)
 
     total = add(uu)
     centre = jnp.where(total > 0, add(uw + ratio * uu) / total, 0.0)
@@ -324,7 +323,7 @@
 
 
 def update_kernel(got, latent, u_in, q_in, z_in, updated, residual, new, left, sems):
-    m0, _, ww, _, wy, centre = (v[:, :1] for v in recentred(got))
+    m0, _, ww, _, wy, centre = recentred(got)
     alpha0 = 1.0 / centre
     norm1 = alpha0 * alpha0 * ww
     beta = norm1 / m0
@@ -350,9 +349,7 @@
 
 
 def gathered(sets, axis):
-    count = lax.axis_size(axis)
-    got = lax.all_to_all(sets.reshape(count, 8, 128), axis, 0, 0)
-    return got.reshape(8 * count, 128)
+    return lax.all_to_all(sets, axis, 0, 0)
 
 
 def body(latent, counts, exposure, region_ids, coefficients):
@@ -410,7 +407,7 @@
     six = vmem((DAYS + 2, FRAME, COLUMNS))
     u, q, z, sets = pl.pallas_call(
         image_kernel,
-        out_shape=(field, field, field, f32(8 * times, 128)),
+        out_shape=(field, field, field, f32(times, 128)),
         in_specs=[VMEM] * 8,
         out_specs=(VMEM,) * 4,
         scratch_shapes=[six] * 4,
@@ -420,7 +417,7 @@
 
     sets = pl.pallas_call(
         regroup_kernel,
-        out_shape=f32(8 * spaces, 128),
+        out_shape=f32(spaces, 128),
         in_specs=[VMEM],
         out_specs=VMEM,
         compiler_params=PARAMS,

time: 74.4 us -> 73.7 us (level)
  blocking collectives: 42.7 us -> 41.5 us
    all_to_all x2, blocking collectives: 42.7 us -> 41.5 us  [gathered(): return lax.all_to_all(sets, axis, 0, 0)]
where the time goes in v6:
time: 73.7 us; the launch traced here: 73.4 us
  blocking collectives  41.5 us (56%)
  starting transfers between devices  13.4 us (18%)
  waiting for transfers between devices  9.69 us (13%)
  Pallas kernels  7.2 us (10%)
  other arithmetic  0.85 us (1%)
    all_to_all x2, blocking collectives, gathered(): return lax.all_to_all(sets, axis, 0, 0)  41.5 us
    ppermute x1, starting transfers between devices, body(): z_second = lax.ppermute(z_second, ('tm', 'space'), turns(1))  7.25 us
    ppermute x1, waiting for transfers between devices, body(): y_got = lax.ppermute(y_msg, 'tm', pairs(times, 1))  6.06 us
    ppermute x1, waiting for transfers between devices, body(): z_second = lax.ppermute(z_second, ('tm', 'space'), turns(1))  3.63 us
    ppermute x1, starting transfers between devices, body(): c_got = lax.ppermute(c_msg, 'tm', pairs(times, 0))  3.56 us
    pallas_call x1, Pallas kernels, body(): pl.pallas_call(image_kernel, out_shape=(field, field, field, f32(times, 1...  2.37 us
    ppermute x1, starting transfers between devices, body(): y_got = lax.ppermute(y_msg, 'tm', pairs(times, 1))  1.92 us
    pallas_call x1, Pallas kernels, body(): pl.pallas_call(intensity_kernel, out_shape=(field, field, field, edge, ed...  1.62 us
  transfers between devices with their start and end apart: 4, of which 2 were waited for; matrix products, arithmetic and copies ran while one was open for 0% of the time, Pallas kernels for 0%

profile of v6, /device:TPU:1, one launch (start us, length us, event | category | flops | bytes accessed | tf_op | source)
XLA Modules:
  0.0 73.4 jit_solution(3533210517127045025)
XLA Ops:
  0.6 0.9 %select_reduce_fusion = f32[8]{0:T(128)S(1)} fusion(f32[16]{0:T(128)} %param.9, s32[8]{0:T(128)} %param.8), kind=kLoop, calls=%fused_computation | loop fusion | flops 376 | bytes 128 | tf_op jit(solution)/shard_map/reduce_sum | solution.py:365
  1.5 0.1 reduce_sum.12.offset
  1.6 1.6 %intensity.1 = (f32[4,32,1024]{2,1,0:T(8,128)S(1)}, f32[4,32,1024]{2,1,0:T(8,128)S(1)}, f32[4,32,1024]{2,1,0:T(8,128)S(1)}, f32[48,1024]{1,0:T(8,128)S(1)}, f32[48,1024]{1,0:T(8,128)S(1)}) custom-call(f32[8,128]{1,0:T(8,128)S(1)} %reduce_sum.12.offset, f32[4,32,1024]{2,1,0:T(8,128)} %latent.3, s32[4,32,1024]{2,1,0:T(8,128)} %counts.1, f32[4,32,1024]{2,1,0:T(8,128)} %exposure.1), custom_call_target="tpu_custom_call" | custom-call | tf_op jit(solution)/shard_map/intensity/pallas_call | solution.py:367
  3.2 0.7 collective-permute-start
  3.9 7.2 %collective-permute-start.1 = (f32[48,1024]{1,0:T(8,128)S(1)}, f32[48,1024]{1,0:T(8,128)S(1)}, u32[]{:S(2)}, u32[]{:S(2)}) collective-permute-start(f32[48,1024]{1,0:T(8,128)S(1)} %get-tuple-element.20), channel_id=1, source_target_pairs={{1,2},{2,1},{3,4},{4,3},{5,6},{6,5},{7,8},{8,7},{9,10},{10,9},{11,... | collective-permute-start | bytes 589832 | tf_op jit(solution)/shard_map/ppermute | solution.py:392
  11.1 0.0 collective-permute-done.z_first
  11.1 3.6 %collective-permute-done.1.z_second = f32[48,1024]{1,0:T(8,128)S(1)} collective-permute-done((f32[48,1024]{1,0:T(8,128)S(1)}, f32[48,1024]{1,0:T(8,128)S(1)}, u32[]{:S(2)}, u32[]{:S(2)}) %collective-permute-start.1) | collective-permute-done | bytes 196640 | tf_op jit(solution)/shard_map/ppermute | solution.py:392
  14.8 1.5 %residual.1 = (f32[4,48,1024]{2,1,0:T(8,128)S(1)}, f32[4,48,1024]{2,1,0:T(8,128)S(1)}, f32[2,48,1024]{2,1,0:T(8,128)S(1)}, f32[152,1024]{1,0:T(8,128)S(1)}, f32[152,1024]{1,0:T(8,128)S(1)}) custom-call(f32[4,32,1024]{2,1,0:T(8,128)S(1)} %get-tuple-element.16.latent, f32[4,32,1024]{2,1,0:T(8,128)S(1)} %get-tuple-element.17.inten, ...), custom_call_target="tpu_custom_call" | custom-call | tf_op jit(solution)/shard_map/residual/pallas_call | solution.py:394
  16.2 1.9 %collective-permute-start.2 = (f32[152,1024]{1,0:T(8,128)S(1)}, f32[152,1024]{1,0:T(8,128)S(1)}, u32[]{:S(2)}, u32[]{:S(2)}) collective-permute-start(f32[152,1024]{1,0:T(8,128)S(1)} %get-tuple-element.24), channel_id=1, source_target_pairs={{16,32},{32,16},{48,64},{64,48},{80,96},{96,80},{112,128},{128,112... | collective-permute-start | bytes 1867784 | tf_op jit(solution)/shard_map/ppermute | solution.py:404
  18.2 3.6 %collective-permute-start.3 = (f32[152,1024]{1,0:T(8,128)S(1)}, f32[152,1024]{1,0:T(8,128)S(1)}, u32[]{:S(2)}, u32[]{:S(2)}) collective-permute-start(f32[152,1024]{1,0:T(8,128)S(1)} %get-tuple-element.25), channel_id=1, source_target_pairs={{0,16},{16,0},{32,48},{48,32},{64,80},{80,64},{96,112},{112,96},{1... | collective-permute-start | bytes 1867784 | tf_op jit(solution)/shard_map/ppermute | solution.py:405
  21.7 6.1 %collective-permute-done.2.y_msg = f32[152,1024]{1,0:T(8,128)S(1)} collective-permute-done((f32[152,1024]{1,0:T(8,128)S(1)}, f32[152,1024]{1,0:T(8,128)S(1)}, u32[]{:S(2)}, u32[]{:S(2)}) %collective-permute-start.2) | collective-permute-done | bytes 622624 | tf_op jit(solution)/shard_map/ppermute | solution.py:404
  27.8 0.0 collective-permute-done.3.c_msg
  27.8 0.0 copy-start
  27.8 2.4 %image.1 = (f32[4,32,1024]{2,1,0:T(8,128)S(1)}, f32[4,32,1024]{2,1,0:T(8,128)S(1)}, f32[4,32,1024]{2,1,0:T(8,128)S(1)}, f32[32,128]{1,0:T(8,128)S(1)}) custom-call(f32[4,48,1024]{2,1,0:T(8,128)S(1)} %get-tuple-element.21.res, f32[2,48,1024]{2,1,0:T(8,128)S(1)} %get-tuple-element.22.inner, f32[4,48,1024]{2,1,0:T(8,128)S(1)} %get-tuple-element.23.lat, ...), custom_call_target="tpu_custom_call" | custom-call | tf_op jit(solution)/shard_map/image/pallas_call | solution.py:408
  30.2 15.3 %all_to_all.22 = f32[32,1,128]{2,1,0:T(1,128)S(1)} all-to-all(f32[32,1,128]{2,1,0:T(1,128)S(1)} %bitcast.11), channel_id=1, replica_groups=mesh['tm'=32,'space'=16] {'tm'}, dimensions={0} | all-to-all | bytes 32768 | tf_op jit(solution)/shard_map/all_to_all | solution.py:352
  45.4 0.3 regroup.1
  45.7 26.2 %all_to_all.23 = f32[16,1,128]{2,1,0:T(1,128)S(1)} all-to-all(f32[16,1,128]{2,1,0:T(1,128)S(1)} %bitcast.10), channel_id=1, replica_groups=mesh['tm'=32,'space'=16] {'space'}, dimensions={0} | all-to-all | bytes 16384 | tf_op jit(solution)/shard_map/all_to_all | solution.py:352
  71.9 0.0 copy-done
  71.9 1.4 %update.1 = (f32[4,32,1024]{2,1,0:T(8,128)}, f32[4,32,1024]{2,1,0:T(8,128)}) custom-call(f32[16,128]{1,0:T(8,128)S(1)} %bitcast.9, f32[4,32,1024]{2,1,0:T(8,128)S(1)} %copy-done, f32[4,32,1024]{2,1,0:T(8,128)S(1)} %get-tuple-element.27.u_in, f32[4,32,1024]{2,1,0:T(8,128)S(1)} %get-tuple-element.28.q_in, f32[4,32,1024]{2,1,0:T(8,128)S(1)} %get-tuple-element.29.z_in), custom_call_target="tpu_custom_call" | custom-call | tf_op jit(solution)/shard_map/update/pallas_call | solution.py:427
Async XLA Ops:
  3.2 7.9 %collective-permute-start = (f32[48,1024]{1,0:T(8,128)S(1)}, f32[48,1024]{1,0:T(8,128)S(1)}, u32[]{:S(2)}, u32[]{:S(2)}) collective-permute-start(f32[48,1024]{1,0:T(8,128)S(1)} %get-tuple-element.19), channel_id=1, source_target_pairs={{0,1},{1,0},{2,3},{3,2},{4,5},{5,4},{6,7},{7,6},{8,9},{9,8},{10,11... | collective-permute-start | bytes 589832 | tf_op jit(solution)/shard_map/ppermute | solution.py:391
  3.9 10.9 %collective-permute-start.1 = (f32[48,1024]{1,0:T(8,128)S(1)}, f32[48,1024]{1,0:T(8,128)S(1)}, u32[]{:S(2)}, u32[]{:S(2)}) collective-permute-start(f32[48,1024]{1,0:T(8,128)S(1)} %get-tuple-element.20), channel_id=1, source_target_pairs={{1,2},{2,1},{3,4},{4,3},{5,6},{6,5},{7,8},{8,7},{9,10},{10,9},{11,... | collective-permute-start | bytes 589832 | tf_op jit(solution)/shard_map/ppermute | solution.py:392
  16.2 11.6 %collective-permute-start.2 = (f32[152,1024]{1,0:T(8,128)S(1)}, f32[152,1024]{1,0:T(8,128)S(1)}, u32[]{:S(2)}, u32[]{:S(2)}) collective-permute-start(f32[152,1024]{1,0:T(8,128)S(1)} %get-tuple-element.24), channel_id=1, source_target_pairs={{16,32},{32,16},{48,64},{64,48},{80,96},{96,80},{112,128},{128,112... | collective-permute-start | bytes 1867784 | tf_op jit(solution)/shard_map/ppermute | solution.py:404
  18.2 9.6 %collective-permute-start.3 = (f32[152,1024]{1,0:T(8,128)S(1)}, f32[152,1024]{1,0:T(8,128)S(1)}, u32[]{:S(2)}, u32[]{:S(2)}) collective-permute-start(f32[152,1024]{1,0:T(8,128)S(1)} %get-tuple-element.25), channel_id=1, source_target_pairs={{0,16},{16,0},{32,48},{48,32},{64,80},{80,64},{96,112},{112,96},{1... | collective-permute-start | bytes 1867784 | tf_op jit(solution)/shard_map/ppermute | solution.py:405
  27.8 44.2 %copy-start = (f32[4,32,1024]{2,1,0:T(8,128)S(1)}, f32[4,32,1024]{2,1,0:T(8,128)}, u32[]{:S(2)}) copy-start(f32[4,32,1024]{2,1,0:T(8,128)} %latent.3) | copy-start | bytes 1572868

commit v7 on v6

--- a/solution.py
+++ b/solution.py
@@ -65,12 +65,12 @@
         return jnp.where(self.which, self.first[at], self.second[at])
 
 
-def alike():
-    return lax.rem(lax.axis_index("space") + lax.axis_index("tm"), 2) == 0
+def unlike():
+    return lax.rem(lax.axis_index("space") + lax.axis_index("tm"), 2) == 1
 
 
 def edges(first, second):
-    return Either(alike(), second, first), Either(alike(), first, second)
+    return Either(unlike(), second, first), Either(unlike(), first, second)
 
 
 def apply_k(load, dst, planes, has_above, has_below, tiles=range(TILES)):
@@ -107,7 +107,7 @@
 def intensity_kernel(
     offset, latent, counts, exposure, lat, exc, inten, z_first, z_second, cnt, exposed, sems
 ):
-    same = alike()
+    same = unlike()
 
     def send(at, tail, head):
         z_first[rows(at), :] = jnp.where(same, tail, head)
@@ -388,8 +388,8 @@
             for i, j in pairs(spaces, (t + k) % 2)
         ]
 
-    z_first = lax.ppermute(z_first, ("tm", "space"), turns(0))
-    z_second = lax.ppermute(z_second, ("tm", "space"), turns(1))
+    z_first = lax.ppermute(z_first, ("tm", "space"), turns(1))
+    z_second = lax.ppermute(z_second, ("tm", "space"), turns(0))
 
     spatial, res, inner, y_msg, c_msg = pl.pallas_call(
         residual_kernel,

time: 73.7 us -> 74.2 us (level)
  starting transfers between devices: 13.4 us -> 15.4 us
  waiting for transfers between devices: 9.69 us -> 8.34 us
    ppermute x1, starting transfers between devices: 1.92 us -> 8.46 us  [body(): y_got = lax.ppermute(y_msg, 'tm', pairs(times, 1))]
    ppermute x2, starting transfers between devices: 7.92 us -> 5.05 us  [the longest x1 4.38 us: body(): z_first = lax.ppermute(z_first, ('tm', 'space'), turns(1))]
    ppermute x1, starting transfers between devices: 3.56 us -> 1.92 us  [body(): c_got = lax.ppermute(c_msg, 'tm', pairs(times, 0))]
    ppermute x2, waiting for transfers between devices: 3.63 us -> 2.37 us  [the longest x1 2.36 us: body(): z_first = lax.ppermute(z_first, ('tm', 'space'), turns(1))]
where the time goes in v7:
time: 74.2 us; the launch traced here: 73.9 us
  blocking collectives  41.3 us (56%)
  starting transfers between devices  15.4 us (21%)
  waiting for transfers between devices  8.34 us (11%)
  Pallas kernels  7.2 us (10%)
  other arithmetic  0.85 us (1%)
    all_to_all x2, blocking collectives, gathered(): return lax.all_to_all(sets, axis, 0, 0)  41.3 us
    ppermute x1, starting transfers between devices, body(): y_got = lax.ppermute(y_msg, 'tm', pairs(times, 1))  8.46 us
    ppermute x1, waiting for transfers between devices, body(): y_got = lax.ppermute(y_msg, 'tm', pairs(times, 1))  5.97 us
    ppermute x1, starting transfers between devices, body(): z_first = lax.ppermute(z_first, ('tm', 'space'), turns(1))  4.38 us
    pallas_call x1, Pallas kernels, body(): pl.pallas_call(image_kernel, out_shape=(field, field, field, f32(times, 1...  2.37 us
    ppermute x1, waiting for transfers between devices, body(): z_first = lax.ppermute(z_first, ('tm', 'space'), turns(1))  2.36 us
    ppermute x1, starting transfers between devices, body(): c_got = lax.ppermute(c_msg, 'tm', pairs(times, 0))  1.92 us
    pallas_call x1, Pallas kernels, body(): pl.pallas_call(intensity_kernel, out_shape=(field, field, field, edge, ed...  1.62 us
  transfers between devices with their start and end apart: 4, of which 2 were waited for; matrix products, arithmetic and copies ran while one was open for 0% of the time, Pallas kernels for 0%

profile of v7, /device:TPU:1, one launch (start us, length us, event | category | flops | bytes accessed | tf_op | source)
XLA Modules:
  0.0 73.9 jit_solution(7048231464587457271)
XLA Ops:
  0.6 0.9 %select_reduce_fusion = f32[8]{0:T(128)S(1)} fusion(f32[16]{0:T(128)} %param.9, s32[8]{0:T(128)} %param.8), kind=kLoop, calls=%fused_computation | loop fusion | flops 376 | bytes 128 | tf_op jit(solution)/shard_map/reduce_sum | solution.py:365
  1.5 0.1 reduce_sum.12.offset
  1.6 1.6 %intensity.1 = (f32[4,32,1024]{2,1,0:T(8,128)S(1)}, f32[4,32,1024]{2,1,0:T(8,128)S(1)}, f32[4,32,1024]{2,1,0:T(8,128)S(1)}, f32[48,1024]{1,0:T(8,128)S(1)}, f32[48,1024]{1,0:T(8,128)S(1)}) custom-call(f32[8,128]{1,0:T(8,128)S(1)} %reduce_sum.12.offset, f32[4,32,1024]{2,1,0:T(8,128)} %latent.3, s32[4,32,1024]{2,1,0:T(8,128)} %counts.1, f32[4,32,1024]{2,1,0:T(8,128)} %exposure.1), custom_call_target="tpu_custom_call" | custom-call | tf_op jit(solution)/shard_map/intensity/pallas_call | solution.py:367
  3.2 4.4 %collective-permute-start = (f32[48,1024]{1,0:T(8,128)S(1)}, f32[48,1024]{1,0:T(8,128)S(1)}, u32[]{:S(2)}, u32[]{:S(2)}) collective-permute-start(f32[48,1024]{1,0:T(8,128)S(1)} %get-tuple-element.19), channel_id=1, source_target_pairs={{1,2},{2,1},{3,4},{4,3},{5,6},{6,5},{7,8},{8,7},{9,10},{10,9},{11,... | collective-permute-start | bytes 589832 | tf_op jit(solution)/shard_map/ppermute | solution.py:391
  7.6 0.7 collective-permute-start.1
  8.3 2.4 %collective-permute-done.z_first = f32[48,1024]{1,0:T(8,128)S(1)} collective-permute-done((f32[48,1024]{1,0:T(8,128)S(1)}, f32[48,1024]{1,0:T(8,128)S(1)}, u32[]{:S(2)}, u32[]{:S(2)}) %collective-permute-start) | collective-permute-done | bytes 196640 | tf_op jit(solution)/shard_map/ppermute | solution.py:391
  10.6 0.0 collective-permute-done.1.z_second
  10.6 1.5 %residual.1 = (f32[4,48,1024]{2,1,0:T(8,128)S(1)}, f32[4,48,1024]{2,1,0:T(8,128)S(1)}, f32[2,48,1024]{2,1,0:T(8,128)S(1)}, f32[152,1024]{1,0:T(8,128)S(1)}, f32[152,1024]{1,0:T(8,128)S(1)}) custom-call(f32[4,32,1024]{2,1,0:T(8,128)S(1)} %get-tuple-element.16.latent, f32[4,32,1024]{2,1,0:T(8,128)S(1)} %get-tuple-element.17.inten, ...), custom_call_target="tpu_custom_call" | custom-call | tf_op jit(solution)/shard_map/residual/pallas_call | solution.py:394
  12.1 8.5 %collective-permute-start.2 = (f32[152,1024]{1,0:T(8,128)S(1)}, f32[152,1024]{1,0:T(8,128)S(1)}, u32[]{:S(2)}, u32[]{:S(2)}) collective-permute-start(f32[152,1024]{1,0:T(8,128)S(1)} %get-tuple-element.24), channel_id=1, source_target_pairs={{16,32},{32,16},{48,64},{64,48},{80,96},{96,80},{112,128},{128,112... | collective-permute-start | bytes 1867784 | tf_op jit(solution)/shard_map/ppermute | solution.py:404
  20.6 1.9 %collective-permute-start.3 = (f32[152,1024]{1,0:T(8,128)S(1)}, f32[152,1024]{1,0:T(8,128)S(1)}, u32[]{:S(2)}, u32[]{:S(2)}) collective-permute-start(f32[152,1024]{1,0:T(8,128)S(1)} %get-tuple-element.25), channel_id=1, source_target_pairs={{0,16},{16,0},{32,48},{48,32},{64,80},{80,64},{96,112},{112,96},{1... | collective-permute-start | bytes 1867784 | tf_op jit(solution)/shard_map/ppermute | solution.py:405
  22.5 6.0 %collective-permute-done.2.y_msg = f32[152,1024]{1,0:T(8,128)S(1)} collective-permute-done((f32[152,1024]{1,0:T(8,128)S(1)}, f32[152,1024]{1,0:T(8,128)S(1)}, u32[]{:S(2)}, u32[]{:S(2)}) %collective-permute-start.2) | collective-permute-done | bytes 622624 | tf_op jit(solution)/shard_map/ppermute | solution.py:404
  28.5 0.0 collective-permute-done.3.c_msg
  28.5 0.0 copy-start
  28.5 2.4 %image.1 = (f32[4,32,1024]{2,1,0:T(8,128)S(1)}, f32[4,32,1024]{2,1,0:T(8,128)S(1)}, f32[4,32,1024]{2,1,0:T(8,128)S(1)}, f32[32,128]{1,0:T(8,128)S(1)}) custom-call(f32[4,48,1024]{2,1,0:T(8,128)S(1)} %get-tuple-element.21.res, f32[2,48,1024]{2,1,0:T(8,128)S(1)} %get-tuple-element.22.inner, f32[4,48,1024]{2,1,0:T(8,128)S(1)} %get-tuple-element.23.lat, ...), custom_call_target="tpu_custom_call" | custom-call | tf_op jit(solution)/shard_map/image/pallas_call | solution.py:408
  30.8 14.4 %all_to_all.22 = f32[32,1,128]{2,1,0:T(1,128)S(1)} all-to-all(f32[32,1,128]{2,1,0:T(1,128)S(1)} %bitcast.11), channel_id=1, replica_groups=mesh['tm'=32,'space'=16] {'tm'}, dimensions={0} | all-to-all | bytes 32768 | tf_op jit(solution)/shard_map/all_to_all | solution.py:352
  45.2 0.3 regroup.1
  45.5 26.9 %all_to_all.23 = f32[16,1,128]{2,1,0:T(1,128)S(1)} all-to-all(f32[16,1,128]{2,1,0:T(1,128)S(1)} %bitcast.10), channel_id=1, replica_groups=mesh['tm'=32,'space'=16] {'space'}, dimensions={0} | all-to-all | bytes 16384 | tf_op jit(solution)/shard_map/all_to_all | solution.py:352
  72.5 0.0 copy-done
  72.5 1.4 %update.1 = (f32[4,32,1024]{2,1,0:T(8,128)}, f32[4,32,1024]{2,1,0:T(8,128)}) custom-call(f32[16,128]{1,0:T(8,128)S(1)} %bitcast.9, f32[4,32,1024]{2,1,0:T(8,128)S(1)} %copy-done, f32[4,32,1024]{2,1,0:T(8,128)S(1)} %get-tuple-element.27.u_in, f32[4,32,1024]{2,1,0:T(8,128)S(1)} %get-tuple-element.28.q_in, f32[4,32,1024]{2,1,0:T(8,128)S(1)} %get-tuple-element.29.z_in), custom_call_target="tpu_custom_call" | custom-call | tf_op jit(solution)/shard_map/update/pallas_call | solution.py:427
Async XLA Ops:
  3.2 7.4 %collective-permute-start = (f32[48,1024]{1,0:T(8,128)S(1)}, f32[48,1024]{1,0:T(8,128)S(1)}, u32[]{:S(2)}, u32[]{:S(2)}) collective-permute-start(f32[48,1024]{1,0:T(8,128)S(1)} %get-tuple-element.19), channel_id=1, source_target_pairs={{1,2},{2,1},{3,4},{4,3},{5,6},{6,5},{7,8},{8,7},{9,10},{10,9},{11,... | collective-permute-start | bytes 589832 | tf_op jit(solution)/shard_map/ppermute | solution.py:391
  7.6 3.0 %collective-permute-start.1 = (f32[48,1024]{1,0:T(8,128)S(1)}, f32[48,1024]{1,0:T(8,128)S(1)}, u32[]{:S(2)}, u32[]{:S(2)}) collective-permute-start(f32[48,1024]{1,0:T(8,128)S(1)} %get-tuple-element.20), channel_id=1, source_target_pairs={{0,1},{1,0},{2,3},{3,2},{4,5},{5,4},{6,7},{7,6},{8,9},{9,8},{10,11... | collective-permute-start | bytes 589832 | tf_op jit(solution)/shard_map/ppermute | solution.py:392
  12.1 16.4 %collective-permute-start.2 = (f32[152,1024]{1,0:T(8,128)S(1)}, f32[152,1024]{1,0:T(8,128)S(1)}, u32[]{:S(2)}, u32[]{:S(2)}) collective-permute-start(f32[152,1024]{1,0:T(8,128)S(1)} %get-tuple-element.24), channel_id=1, source_target_pairs={{16,32},{32,16},{48,64},{64,48},{80,96},{96,80},{112,128},{128,112... | collective-permute-start | bytes 1867784 | tf_op jit(solution)/shard_map/ppermute | solution.py:404
  20.6 7.9 %collective-permute-start.3 = (f32[152,1024]{1,0:T(8,128)S(1)}, f32[152,1024]{1,0:T(8,128)S(1)}, u32[]{:S(2)}, u32[]{:S(2)}) collective-permute-start(f32[152,1024]{1,0:T(8,128)S(1)} %get-tuple-element.25), channel_id=1, source_target_pairs={{0,16},{16,0},{32,48},{48,32},{64,80},{80,64},{96,112},{112,96},{1... | collective-permute-start | bytes 1867784 | tf_op jit(solution)/shard_map/ppermute | solution.py:405
  28.5 44.0 %copy-start = (f32[4,32,1024]{2,1,0:T(8,128)S(1)}, f32[4,32,1024]{2,1,0:T(8,128)}, u32[]{:S(2)}) copy-start(f32[4,32,1024]{2,1,0:T(8,128)} %latent.3) | copy-start | bytes 1572868
